TPU v7x, 512 devices: a whole 4x8x8 slice. The times are simulated.
512 devices in a mesh: section: 16 (over y_lo, z), seq: 32 (over x, y_hi, core).
Axes of the slice: x: 4, y: 8 (y_hi: 4, y_lo: 2; y = y_hi * 2 + y_lo), z: 8, core: 2. Of those that a mesh axis runs over, the one named last changes fastest.
Arguments:
- codes_fwd: bfloat16 [16, 4096, 512], P('section', 'seq'), may hold values from -0.29882812 to 0.29882812
- saved_stream: bfloat16 [16, 4096, 4096], P('section', 'seq'), may hold values from -0.29882812 to 0.29882812
- grad_codes: bfloat16 [16, 4096, 512], P('section', 'seq'), may hold values from -0.29882812 to 0.29882812
- docs_fwd: int32 [16, 4096], P('section', 'seq'), may hold values from 0 to 1, never falling along the last dimension, each value on 1 to 3584 neighbouring positions
- docs_bwd: int32 [16, 4096], P('section', 'seq'), may hold values from 0 to 1, never falling along the last dimension, each value on 1 to 3584 neighbouring positions
- codec: bfloat16 [4096, 512], P(('section', 'seq')), may hold values from -0.25 to 0.25
- wqkv: bfloat16 [16, 4096, 512], P('section', 'seq'), may hold values from -2 to 2
- wout: bfloat16 [16, 4096, 256], P('section', 'seq'), may hold values from -0.375 to 0.375
- gain_attn: bfloat16 [16, 4096], P('section', 'seq'), may hold values from 0.099609375 to 1.8984375
- gain_code: bfloat16 [16, 4096], P('section', 'seq'), may hold values from 0.099609375 to 1.8984375
Outputs:
- codes_next: bfloat16 [16, 4096, 512], P('section', 'seq')
- grads_next: bfloat16 [16, 4096, 512], P('section', 'seq')
Inputs may be any that keep to these rules, and one draw needn't show every extreme that they name: `docs_fwd`: ids never fall along a sequence; each document has at most 3584 tokens. `docs_bwd`: ids never fall along a sequence; each document has at most 3584 tokens.
All inputs are finite; a program needn't handle non-finite values.
Results may differ from a plain program's by a relative error of at most 0.023.
Values may be sent and summed in bfloat16 or wider, within the bound.
A program may use at most 128 MiB of HBM per device.

v0:
```python
import jax
import jax.numpy as jnp
from jax import lax
from jax.sharding import PartitionSpec as P

D = 4096
R = 512
HD = 128
HQ = 2


EPS = 1e-05


def shifted(value, axis, steps):
    count = lax.axis_size(axis)
    pairs = [(source, (source + steps) % count) for source in range(count)]
    return lax.ppermute(value, axis, pairs)


def rms_factor(values):
    return lax.rsqrt(jnp.mean(values * values, axis=-1, keepdims=True) + EPS)


def to_heads(matrix, rows):
    return matrix.reshape(rows, HQ, HD).transpose(1, 0, 2)


def from_heads(heads, rows):
    return heads.transpose(1, 0, 2).reshape(rows, HQ * HD)


def on_device(
    codes_fwd, saved_stream, grad_codes, docs_fwd, docs_bwd, codec, wqkv, wout, gain_attn, gain_code
):
    rows = codes_fwd.shape[1]
    qwidth = HQ * HD
    scale = HD ** (-0.5)
    enc_scale = (R / D) ** 0.5
    w_all, o_all, g_attn, g_code = (
        lax.all_gather(wqkv, "seq", axis=1, tiled=True),
        lax.all_gather(wout, "seq", axis=1, tiled=True),
        lax.all_gather(gain_attn, "seq", axis=1, tiled=True),
        lax.all_gather(gain_code, "seq", axis=1, tiled=True),
    )
    w_all = w_all[0]
    o_all = o_all[0]
    g_attn = g_attn[0]
    g_code = g_code[0]
    codec_all = lax.all_gather(codec, ("section", "seq"), axis=0, tiled=True)
    place = lax.axis_index("seq") * rows + jnp.arange(rows, dtype=jnp.int32)
    contract_last = (((1,), (1,)), ((), ()))

    def project(stream):
        scale1 = rms_factor(stream)
        normed = (stream * scale1 * g_attn).astype(jnp.bfloat16)
        qkv = jnp.dot(normed, w_all, preferred_element_type=jnp.float32).astype(jnp.bfloat16)
        queries = to_heads(qkv[:, :qwidth], rows)
        return (scale1, queries, qkv[:, qwidth : qwidth + HD], qkv[:, qwidth + HD :])

    def finish_forward(stream, attended):
        return stream + lax.dot_general(
            attended, o_all, contract_last, preferred_element_type=jnp.float32
        )

    stream = lax.dot_general(
        codes_fwd[0], codec_all, contract_last, preferred_element_type=jnp.float32
    )
    scale1, queries, keys, values = project(stream)
    docs = docs_fwd[0]
    top = jnp.full((HQ, rows), -1e30, jnp.float32)
    piece_k = lax.all_gather(keys, "seq", axis=0, tiled=True)
    piece_v = lax.all_gather(values, "seq", axis=0, tiled=True)
    piece_d = lax.all_gather(docs, "seq", axis=0, tiled=True)
    k_pos = jnp.arange(piece_k.shape[0], dtype=jnp.int32)
    allowed = ((k_pos[None, :] <= place[:, None]) & (piece_d[None, :] == docs[:, None]))[None]
    scores = jnp.einsum("htd,sd->hts", queries, piece_k, preferred_element_type=jnp.float32) * scale
    masked = jnp.where(allowed, scores, -1e30)
    new_top = jnp.maximum(top, jnp.max(masked, axis=-1))
    probs = jnp.where(allowed, jnp.exp(masked - new_top[..., None]), 0.0)
    total = jnp.sum(probs, axis=-1)
    accum = jnp.einsum(
        "hts,sd->htd", probs.astype(jnp.bfloat16), piece_v, preferred_element_type=jnp.float32
    )
    top, total, accum = (new_top, total, accum)
    attended = from_heads(accum / total[..., None], rows).astype(jnp.bfloat16)
    mixed = finish_forward(stream, attended)
    normed = (mixed * rms_factor(mixed) * g_code).astype(jnp.bfloat16)
    coded = (jnp.dot(normed, codec_all, preferred_element_type=jnp.float32) * enc_scale).astype(
        jnp.bfloat16
    )
    codes_out = shifted(coded, "section", 1)
    stream = saved_stream[0].astype(jnp.float32)
    scale1, backward_queries, keys, values = project(stream)
    backward_docs = docs_bwd[0]
    all_keys = lax.all_gather(keys, "seq", axis=0, tiled=True)
    all_values = lax.all_gather(values, "seq", axis=0, tiled=True)
    all_docs = lax.all_gather(backward_docs, "seq", axis=0, tiled=True)
    k_pos = jnp.arange(all_keys.shape[0], dtype=jnp.int32)
    allowed = ((k_pos[None, :] <= place[:, None]) & (all_docs[None, :] == backward_docs[:, None]))[
        None
    ]
    scores = (
        jnp.einsum("htd,sd->hts", backward_queries, all_keys, preferred_element_type=jnp.float32)
        * scale
    )
    masked = jnp.where(allowed, scores, -1e30)
    top = jnp.max(masked, axis=-1, keepdims=True)
    probs = jnp.where(allowed, jnp.exp(masked - top), 0.0)
    denom = jnp.sum(probs, axis=-1, keepdims=True)
    summed = jnp.einsum(
        "hts,sd->htd", probs.astype(jnp.bfloat16), all_values, preferred_element_type=jnp.float32
    )
    attended_heads = (summed / denom).astype(jnp.bfloat16)
    attended = from_heads(attended_heads, rows)
    mixed = finish_forward(stream, attended)
    scale2 = rms_factor(mixed)
    pre2 = mixed * scale2
    grad_n2 = (
        lax.dot_general(grad_codes[0], codec_all, contract_last, preferred_element_type=jnp.float32)
        * enc_scale
    )
    weighted2 = grad_n2 * g_code
    grad_mixed = scale2 * (weighted2 - pre2 * jnp.mean(weighted2 * pre2, axis=-1, keepdims=True))
    grad_att = jnp.dot(
        grad_mixed.astype(jnp.bfloat16), o_all, preferred_element_type=jnp.float32
    ).astype(jnp.bfloat16)
    grad_heads = to_heads(grad_att, rows)
    grad_p = jnp.einsum("htd,sd->hts", grad_heads, all_values, preferred_element_type=jnp.float32)
    delta = jnp.einsum(
        "htd,htd->ht", grad_heads.astype(jnp.float32), attended_heads.astype(jnp.float32)
    )
    grad_s = (probs / denom * (grad_p - delta[..., None]) * scale).astype(jnp.bfloat16)
    probs_b = (probs / denom).astype(jnp.bfloat16)
    grad_q = from_heads(
        jnp.einsum("hts,sd->htd", grad_s, all_keys, preferred_element_type=jnp.float32), rows
    )
    key_term = jnp.einsum(
        "hts,htd->sd", grad_s, backward_queries, preferred_element_type=jnp.float32
    )
    value_term = jnp.einsum("hts,htd->sd", probs_b, grad_heads, preferred_element_type=jnp.float32)
    kv_grad = lax.psum_scatter(
        jnp.concatenate([key_term, value_term], axis=1).astype(jnp.bfloat16),
        "seq",
        scatter_dimension=0,
        tiled=True,
    ).astype(jnp.float32)
    grad_qkv = jnp.concatenate([grad_q, kv_grad], axis=1).astype(jnp.bfloat16)
    grad_n1 = lax.dot_general(grad_qkv, w_all, contract_last, preferred_element_type=jnp.float32)
    pre1 = stream * scale1
    weighted1 = grad_n1 * g_attn
    grad_stream = grad_mixed + scale1 * (
        weighted1 - pre1 * jnp.mean(weighted1 * pre1, axis=-1, keepdims=True)
    )
    grad_in = jnp.dot(
        grad_stream.astype(jnp.bfloat16), codec_all, preferred_element_type=jnp.float32
    ).astype(jnp.bfloat16)
    grads_out = shifted(grad_in, "section", -1)
    return (codes_out[None], grads_out[None])


def solution(mesh):
    return jax.shard_map(
        on_device,
        mesh=mesh,
        in_specs=(
            P("section", "seq", None),
            P("section", "seq", None),
            P("section", "seq", None),
            P("section", "seq"),
            P("section", "seq"),
            P(("section", "seq"), None),
            P("section", "seq", None),
            P("section", "seq", None),
            P("section", "seq"),
            P("section", "seq"),
        ),
        out_specs=(P("section", "seq", None), P("section", "seq", None)),
        check_vma=False,
    )
```

profile of v0, /device:TPU:1, one launch (start us, length us, event | category | flops | bytes accessed | tf_op | source)
XLA Modules:
  0.0 1308.1 jit_solution(8444723269239388885)
XLA Ops:
  8.7 46.5 %all_gather.35 = bf16[1,4096]{1,0:T(2,128)(2,1)S(1)} all-gather(bf16[1,128]{1,0:T(2,128)(2,1)} %param.18), channel_id=1, replica_groups=mesh['section'=16,'seq'=32] {'seq'}, dimensions={1}, use_global_device_ids=true | all-gather | bytes 8448 | tf_op jit(solution)/shard_map/all_gather | solution.py:43
  56.8 25.9 %all-gather.12.cloned.1.call-done = bf16[1,4096,512]{2,1,0:T(8,128)(2,1)} async-done(((bf16[1,128,512]{2,1,0:T(8,128)(2,1)}), bf16[1,4096,512]{2,1,0:T(8,128)(2,1)}) %all-gather.12.cloned.1.call-update) | async-done | bytes 4194320 | tf_op jit(solution)/shard_map/all_gather | solution.py:41
  82.7 3.3 fusion.47
  87.9 796.5 %all-gather.10.cloned.1.call-done = bf16[4096,512]{1,0:T(8,128)(2,1)} async-done(((bf16[8,512]{1,0:T(8,128)(2,1)}), bf16[4096,512]{1,0:T(8,128)(2,1)}) %all-gather.10.cloned.1.call-update) | async-done | bytes 4194320 | tf_op jit(solution)/shard_map/all_gather | solution.py:50
  884.4 3.9 multiply_reduce_fusion.3
  890.4 46.5 %all_gather.40 = bf16[1,4096]{1,0:T(2,128)(2,1)S(1)} all-gather(bf16[1,128]{1,0:T(2,128)(2,1)S(1)} %copy-done.34), channel_id=1, replica_groups=mesh['section'=16,'seq'=32] {'seq'}, dimensions={1}, use_global_device_ids=true | all-gather | bytes 8448 | tf_op jit(solution)/shard_map/all_gather | solution.py:44
  936.9 40.6 %all-gather = s32[1,4096]{1,0:T(1,128)S(1)} all-gather(s32[1,128]{1,0:T(1,128)S(1)} %copy-done.31), channel_id=2, replica_groups=mesh['section'=16,'seq'=32] {'seq'}, dimensions={1}, use_global_device_ids=true | all-gather | bytes 16896 | tf_op jit(solution)/shard_map/all_gather | solution.py:74
  977.5 39.5 %all-gather.1 = s32[1,4096]{1,0:T(1,128)S(1)} all-gather(s32[1,128]{1,0:T(1,128)S(1)} %copy-done.30), channel_id=3, replica_groups=mesh['section'=16,'seq'=32] {'seq'}, dimensions={1}, use_global_device_ids=true | all-gather | bytes 16896 | tf_op jit(solution)/shard_map/all_gather | solution.py:98
  1019.6 5.3 fusion.111
  1024.9 4.0 fusion.88
  1029.0 40.6 %all-gather.18.cloned.1.call-done = bf16[1,4096,256]{2,1,0:T(8,128)(2,1)} async-done(((bf16[1,128,256]{2,1,0:T(8,128)(2,1)}), bf16[1,4096,256]{2,1,0:T(8,128)(2,1)}) %all-gather.18.cloned.1.call-update) | async-done | bytes 2097168 | tf_op jit(solution)/shard_map/all_gather | solution.py:42
  1069.6 2.7 multiply_reduce_fusion.1
  1079.2 3.3 fusion.8
  1087.6 4.1 copy.34
  1091.7 2.7 convolution_convert_fusion.1
  1094.4 32.9 %all-gather.14.cloned.1.call-done = bf16[4096,128]{1,0:T(8,128)(2,1)} async-done(((bf16[128,128]{1,0:T(8,128)(2,1)}), bf16[4096,128]{1,0:T(8,128)(2,1)}) %all-gather.14.cloned.1.call-update) | async-done | bytes 1048592 | tf_op jit(solution)/shard_map/all_gather | solution.py:72
  1127.4 2.5 fusion.110
  1129.8 2.0 copy-done.12
  1132.9 52.8 %all-gather.16.cloned.1.call-done = bf16[4096,128]{1,0:T(8,128)(2,1)} async-done(((bf16[128,128]{1,0:T(8,128)(2,1)}), bf16[4096,128]{1,0:T(8,128)(2,1)}) %all-gather.16.cloned.1.call-update) | async-done | bytes 1048592 | tf_op jit(solution)/shard_map/all_gather | solution.py:73
  1185.7 4.1 fusion.63
  1193.5 3.3 collective-permute-start
  1196.8 88.6 %reduce-scatter.4.cloned.1.call-done = bf16[128,256]{1,0:T(8,128)(2,1)} async-done(((bf16[4096,256]{1,0:T(8,128)(2,1)}), bf16[128,256]{1,0:T(8,128)(2,1)}) %reduce-scatter.4.cloned.1.call-update) | async-done | bytes 65552
  1286.4 4.0 fusion.22
  1291.5 5.6 collective-permute-start.1
  (120 shorter events, 32.4 us)
Async XLA Ops:
  7.2 877.2 %copy-start = (bf16[1,128,512]{2,1,0:T(8,128)(2,1)S(1)}, bf16[1,128,512]{2,1,0:T(8,128)(2,1)}, u32[]{:S(2)}) copy-start(bf16[1,128,512]{2,1,0:T(8,128)(2,1)} %param.10) | copy-start | bytes 393220
  7.2 75.5 %all-gather.12.cloned.1.call-start = ((), (), s32[]{:S(2)}) async-start(), calls=%async_computation.2 | async-start | bytes 4325376 | tf_op jit(solution)/shard_map/all_gather | solution.py:41
  7.9 876.5 %all-gather.10.cloned.1.call-start = ((), (), s32[]{:S(2)}) async-start(), calls=%async_computation.1 | async-start | bytes 4202496 | tf_op jit(solution)/shard_map/all_gather | solution.py:50
  8.7 1010.9 %all-gather.20.cloned.1.call-start = ((), (), s32[]{:S(2)}) async-start(), calls=%async_computation.6 | async-start | bytes 1081344 | tf_op jit(solution)/shard_map/all_gather | solution.py:96
  56.8 29.2 %copy-start.28 = (f32[128]{0:T(128)}, f32[128]{0:T(128)S(1)}, u32[]{:S(2)}) copy-start(f32[128]{0:T(128)S(1)} %add_rsqrt_fusion.1) | copy-start | bytes 1540
  86.0 933.6 %copy-start.21 = (bf16[128,512]{1,0:T(8,128)(2,1)}, bf16[128,512]{1,0:T(8,128)(2,1)S(1)}, u32[]{:S(2)}) copy-start(bf16[128,512]{1,0:T(8,128)(2,1)S(1)} %fusion.47) | copy-start | bytes 393220
  86.7 938.2 %all-gather.22.cloned.1.call-start = ((), (), s32[]{:S(2)}) async-start(), calls=%async_computation.7 | async-start | bytes 1081344 | tf_op jit(solution)/shard_map/all_gather | solution.py:97
  87.3 982.3 %all-gather.18.cloned.1.call-start = ((), (), s32[]{:S(2)}) async-start(), calls=%async_computation.5 | async-start | bytes 2162688 | tf_op jit(solution)/shard_map/all_gather | solution.py:42
  87.8 1039.5 %all-gather.14.cloned.1.call-start = ((), (), s32[]{:S(2)}) async-start(), calls=%async_computation.3 | async-start | bytes 1081344 | tf_op jit(solution)/shard_map/all_gather | solution.py:72
  888.3 48.6 %copy-start.31 = (s32[1,128]{1,0:T(1,128)S(1)}, s32[1,128]{1,0:T(1,128)}, u32[]{:S(2)}) copy-start(s32[1,128]{1,0:T(1,128)} %param.13) | copy-start | bytes 1540
  888.3 89.1 %copy-start.30 = (s32[1,128]{1,0:T(1,128)S(1)}, s32[1,128]{1,0:T(1,128)}, u32[]{:S(2)}) copy-start(s32[1,128]{1,0:T(1,128)} %param.14) | copy-start | bytes 1540
  890.3 295.4 %all-gather.16.cloned.1.call-start = ((), (), s32[]{:S(2)}) async-start(), calls=%async_computation.4 | async-start | bytes 1081344 | tf_op jit(solution)/shard_map/all_gather | solution.py:73
  936.9 88.0 %copy-start.18 = (f32[1,4096]{1,0:T(1,128)}, f32[1,4096]{1,0:T(1,128)S(1)}, u32[]{:S(2)}) copy-start(f32[1,4096]{1,0:T(1,128)S(1)} %mul.208) | copy-start | bytes 49156
  1019.3 266.1 %reduce-scatter.4.cloned.1.call-start = ((), (), s32[]{:S(2)}) async-start(), calls=%async_computation.8 | async-start | bytes 2162688
  1024.9 44.6 %copy-start.13 = (bf16[1,128,4096]{2,1,0:T(8,128)(2,1)S(1)}, bf16[1,128,4096]{2,1,0:T(8,128)(2,1)}, u32[]{:S(2)}) copy-start(bf16[1,128,4096]{2,1,0:T(8,128)(2,1)} %param.11) | copy-start | bytes 3145732
  1127.4 4.4 copy-start.14
  1185.7 4.1 copy-start.5
  1185.7 4.1 copy-start.9
  1192.0 94.3 %copy-start.29 = (f32[128]{0:T(128)S(1)}, f32[128]{0:T(128)}, u32[]{:S(2)}) copy-start(f32[128]{0:T(128)} %copy-done.28) | copy-start | bytes 1540
  1193.5 103.6 %collective-permute-start = (bf16[128,512]{1,0:T(8,128)(2,1)}, bf16[128,512]{1,0:T(8,128)(2,1)}, u32[]{:S(2)}, u32[]{:S(2)}) collective-permute-start(bf16[128,512]{1,0:T(8,128)(2,1)} %fusion.50), channel_id=1, source_target_pairs={{0,32},{32,64},{64,96},{96,128},{128,160},{160,192},{192,224},{224... | collective-permute-start | bytes 393224 | tf_op jit(solution)/shard_map/ppermute | solution.py:18
  1286.3 4.1 copy-start.7
  1286.3 4.1 copy-start.25
  1286.4 4.1 copy-start.33
  1291.5 7.6 collective-permute-start.1
  (21 other events, 50.6 us)
Sparse Core Ops, SparseCore 0:
  11.1 71.5 all-gather.11
  84.9 799.4 all-gather.9
  888.1 62.1 all-gather.19
  953.8 55.2 all-gather.21
  1012.1 57.4 all-gather.17
  1072.5 54.7 all-gather.13
  1130.5 55.1 all-gather.15
  1190.1 95.2 reduce-scatter.3
where the time goes:
time: 1310 us
  waiting for transfers between devices  1040 us (79%)
  blocking collectives  173 us (13%)
  matrix products  43.1 us (3%)
  local copies, waits for them, and re-layouts  18.1 us (1%)
  between operations  14.6 us (1%)
    all_gather x1, waiting for transfers between devices, on_device(): codec_all = lax.all_gather(codec, ('section', 'seq'), axis=0, tiled=True)  796 us
    unnamed x9, waiting for transfers between devices  91.1 us
    all_gather x1, waiting for transfers between devices, on_device(): piece_v = lax.all_gather(values, 'seq', axis=0, tiled=True)  52.8 us
    all_gather x1, blocking collectives, on_device(): lax.all_gather(gain_attn, 'seq', axis=1, tiled=True)  46.5 us
    all_gather x1, blocking collectives, on_device(): lax.all_gather(gain_code, 'seq', axis=1, tiled=True)  46.5 us
    all_gather x1, blocking collectives, on_device(): piece_d = lax.all_gather(docs, 'seq', axis=0, tiled=True)  40.6 us
    all_gather x1, waiting for transfers between devices, on_device(): lax.all_gather(wout, 'seq', axis=1, tiled=True)  40.6 us
    all_gather x1, blocking collectives, on_device(): all_docs = lax.all_gather(backward_docs, 'seq', axis=0, tiled=True)  39.5 us
  transfers between devices with their start and end apart: 10, of which 7 were waited for; matrix products, arithmetic and copies ran while one was open for 5% of the time, Pallas kernels for 0%

commit v1 on v0

v1 whole, which is shorter than its diff:
```python
import functools

import jax
import jax.numpy as jnp
from jax import lax
from jax.experimental import pallas as pl
from jax.experimental.pallas import tpu as pltpu
from jax.sharding import PartitionSpec as P

D = 4096
R = 512
HD = 128
HQ = 2
TOK = 128
QKV = (HQ + 2) * HD
QW = HQ * HD
WCAT = QKV + QW
NX, NYH, NC = 4, 4, 2
NYL, NZ = 2, 8
NSEQ = NX * NYH * NC

EPS = 1e-05


class Place:
    def __init__(self):
        self.section = lax.axis_index("section")
        self.seq = lax.axis_index("seq")
        self.ylo = self.section // NZ
        self.z = lax.rem(self.section, NZ)
        self.x = self.seq // (NYH * NC)
        self.yh = lax.rem(self.seq // NC, NYH)
        self.c = lax.rem(self.seq, NC)

    def slot(self, dx=0, dy=0, dc=0):
        x = lax.rem(self.x + (dx + NX), NX)
        yh = lax.rem(self.yh + (dy + NYH), NYH)
        c = lax.rem(self.c + dc, NC)
        return (x * NYH + yh) * NC + c

    def chip(self, dx=0, dy=0):
        return lax.rem(self.x + (dx + NX), NX) * NYH + lax.rem(self.yh + (dy + NYH), NYH)

    def device(self, dx=0, dy=0, dc=0, dz=0, dyl=0):
        z = lax.rem(self.z + (dz + NZ), NZ)
        ylo = lax.rem(self.ylo + dyl, NYL)
        return {"section": ylo * NZ + z, "seq": self.slot(dx, dy, dc)}


class Wire:
    def __init__(self, send_sems, recv_sems):
        self.send_sems, self.recv_sems = send_sems, recv_sems
        self.started = []

    def send(self, src, dst, device):
        k = len(self.started)
        copy = pltpu.make_async_remote_copy(
            src_ref=src,
            dst_ref=dst,
            send_sem=self.send_sems.at[k],
            recv_sem=self.recv_sems.at[k],
            device_id=device,
            device_id_type=pl.DeviceIdType.MESH,
        )
        copy.start()
        self.started.append(copy)
        return k

    def arrived(self, k, dst):
        pltpu.make_async_copy(dst, dst, self.recv_sems.at[k]).wait()

    def finish(self):
        for copy in self.started:
            copy.wait_send()


def meet(devices):
    barrier = pltpu.get_barrier_semaphore()
    for device in devices:
        pl.semaphore_signal(barrier, inc=1, device_id=device, device_id_type=pl.DeviceIdType.MESH)
    pl.semaphore_wait(barrier, len(devices))


class SectionGather:
    def __init__(self, me, wire, out, rows):
        self.me, self.wire, self.out = me, wire, out
        self.half = rows // 2
        self.sib = []
        self.keys = {}

    def block(self, dx, dy):
        return self.out.at[self.me.slot(dx, dy)]

    def part(self, dx, dy, which):
        return self.out.at[self.me.slot(dx, dy), pl.ds(which * self.half, self.half)]

    def to_sibling(self, dx, dy):
        ref = self.block(dx, dy)
        k = self.wire.send(ref, ref, self.me.device(dc=1))
        self.sib.append((k, dx, dy))

    def begin(self):
        own = self.block(0, 0)
        self.keys["y+"] = self.wire.send(own, own, self.me.device(dy=1))
        self.keys["y-"] = self.wire.send(own, own, self.me.device(dy=-1))
        self.along_x(0)
        self.to_sibling(0, 0)

    def along_x(self, dy):
        ref = self.block(0, dy)
        self.keys["x+", dy] = self.wire.send(ref, ref, self.me.device(dx=1))
        self.keys["x-", dy] = self.wire.send(ref, ref, self.me.device(dx=-1))

    def y_near(self):
        self.wire.arrived(self.keys["y+"], self.block(0, -1))
        ref = self.part(0, -1, 0)
        self.keys["y++"] = self.wire.send(ref, ref, self.me.device(dy=1))
        self.along_x(-1)
        self.wire.arrived(self.keys["y-"], self.block(0, 1))
        ref = self.part(0, 1, 1)
        self.keys["y--"] = self.wire.send(ref, ref, self.me.device(dy=-1))
        self.along_x(1)
        self.to_sibling(0, -1)
        self.to_sibling(0, 1)

    def y_far(self):
        self.wire.arrived(self.keys["y++"], self.part(0, 2, 0))
        self.wire.arrived(self.keys["y--"], self.part(0, 2, 1))
        self.along_x(2)
        self.to_sibling(0, 2)

    def x_near(self, dy):
        self.wire.arrived(self.keys["x+", dy], self.block(-1, dy))
        ref = self.part(-1, dy, 0)
        self.keys["x++", dy] = self.wire.send(ref, ref, self.me.device(dx=1))
        self.wire.arrived(self.keys["x-", dy], self.block(1, dy))
        ref = self.part(1, dy, 1)
        self.keys["x--", dy] = self.wire.send(ref, ref, self.me.device(dx=-1))
        self.to_sibling(-1, dy)
        self.to_sibling(1, dy)

    def x_far(self, dy):
        self.wire.arrived(self.keys["x++", dy], self.part(2, dy, 0))
        self.wire.arrived(self.keys["x--", dy], self.part(2, dy, 1))
        self.to_sibling(2, dy)

    def end(self):
        for k, dx, dy in self.sib:
            self.wire.arrived(k, self.out.at[self.me.slot(dx, dy, 1)])

    def partners(self):
        me = self.me
        return [
            me.device(dy=1),
            me.device(dy=-1),
            me.device(dx=1),
            me.device(dx=-1),
            me.device(dc=1),
        ]


CROWS = 16
PLANE = NX * NYH * CROWS
LANES = R // NC


class CodecGather:
    def __init__(self, me, wire, out, both, other, tile):
        self.me, self.wire, self.out = me, wire, out
        self.both, self.other, self.tile = both, other, tile

    def ref(self, first, rows, dc=0):
        c = lax.rem(self.me.c + dc, NC)
        return self.out.at[
            pl.ds(pl.multiple_of(first, CROWS), rows),
            pl.ds(pl.multiple_of(c * LANES, LANES), LANES),
        ]

    def plane_first(self, dyl, dz):
        me = self.me
        ylo = lax.rem(me.ylo + dyl, NYL)
        return (ylo * NZ + lax.rem(me.z + (dz + NZ), NZ)) * PLANE

    def tile_ref(self, dyl, dy):
        return self.ref(self.plane_first(dyl, 0) + self.me.chip(0, dy) * CROWS, CROWS)

    def column_ref(self, dyl, dx):
        x = lax.rem(self.me.x + (dx + NX), NX)
        return self.ref(self.plane_first(dyl, 0) + x * (NYH * CROWS), NYH * CROWS)

    def plane_ref(self, dyl, dz, dc=0):
        return self.ref(self.plane_first(dyl, dz), PLANE, dc)

    def begin(self):
        self.k_pair = self.wire.send(self.both, self.other, self.me.device(dc=1))

    def pair(self, local_sem):
        me = self.me
        self.wire.arrived(self.k_pair, self.other)
        row = lax.broadcasted_iota(jnp.int32, (CROWS, R), 0)
        mine = (row // (CROWS // NC)) == me.c
        self.tile[...] = jnp.where(
            mine, self.both[...].astype(jnp.float32), self.other[...].astype(jnp.float32)
        ).astype(jnp.bfloat16)
        src = self.tile.at[:, pl.ds(pl.multiple_of(me.c * LANES, LANES), LANES)]
        self.local = pltpu.make_async_copy(src, self.tile_ref(0, 0), local_sem)
        self.local.start()
        self.k_y = []
        for dyl in range(NYL):
            for dy in range(NYH):
                if dyl or dy:
                    k = self.wire.send(src, self.tile_ref(0, 0), me.device(dy=dy, dyl=dyl))
                    self.k_y.append((k, dyl, dy))

    def columns(self):
        me = self.me
        self.local.wait()
        for k, dyl, dy in self.k_y:
            self.wire.arrived(k, self.tile_ref(dyl, -dy))
        self.k_x = []
        for dx in (1, -1, 2):
            for dyl in range(NYL):
                ref = self.column_ref(dyl, 0)
                self.k_x.append((self.wire.send(ref, ref, me.device(dx=dx)), dyl, dx))

    def planes(self):
        for k, dyl, dx in self.k_x:
            self.wire.arrived(k, self.column_ref(dyl, -dx))
        self.k_up, self.k_down, self.sib = {}, {}, []
        for dyl in range(NYL):
            self.pass_on(dyl, 0)

    def pass_on(self, dyl, step):
        me = self.me
        below, above = self.plane_ref(dyl, -step), self.plane_ref(dyl, step)
        if step < NZ // 2 - 1 or (step == NZ // 2 - 1 and dyl == 0):
            self.k_up[dyl, step] = self.wire.send(below, below, me.device(dz=1))
        if step < NZ // 2 - 1 or (step == NZ // 2 - 1 and dyl == 1):
            self.k_down[dyl, step] = self.wire.send(above, above, me.device(dz=-1))
        self.to_sibling(dyl, -step)
        if step:
            self.to_sibling(dyl, step)

    def to_sibling(self, dyl, dz):
        ref = self.plane_ref(dyl, dz)
        self.sib.append((self.wire.send(ref, ref, self.me.device(dc=1)), dyl, dz))

    def step(self, step):
        for dyl in range(NYL):
            if step < NZ // 2:
                self.wire.arrived(self.k_up[dyl, step - 1], self.plane_ref(dyl, -step))
                self.wire.arrived(self.k_down[dyl, step - 1], self.plane_ref(dyl, step))
                self.pass_on(dyl, step)
            else:
                keys = self.k_up if dyl == 0 else self.k_down
                self.wire.arrived(keys[dyl, step - 1], self.plane_ref(dyl, step))
                self.to_sibling(dyl, step)

    def end(self):
        for k, dyl, dz in self.sib:
            self.wire.arrived(k, self.plane_ref(dyl, dz, 1))

    def partners(self):
        me = self.me
        return [
            me.device(dy=2),
            me.device(dx=2),
            me.device(dz=1),
            me.device(dz=-1),
        ] + [me.device(dyl=1, dy=dy) for dy in range(NYH)]


def weights_kernel(
    codec_ref, wqkv_ref, wout_ref, docs_f_ref, docs_b_ref, g1_ref, g2_ref,
    codec_out, w_out, meta_out,
    both, other, tile, meta, send_sems, recv_sems, local_sems,
):
    me = Place()
    wire = Wire(send_sems, recv_sems)
    weights = SectionGather(me, wire, w_out, TOK)
    codec = CodecGather(me, wire, codec_out, both, other, tile)
    own = me.slot()
    fills = [
        pltpu.make_async_copy(wqkv_ref.at[0], w_out.at[own, :, pl.ds(0, QKV)], local_sems.at[0]),
        pltpu.make_async_copy(wout_ref.at[0], w_out.at[own, :, pl.ds(QKV, QW)], local_sems.at[1]),
    ]
    for fill in fills:
        fill.start()
    rows = codec_ref[...].astype(jnp.float32)
    both[...] = jnp.concatenate([rows, rows], axis=0).astype(jnp.bfloat16)
    meta[...] = jnp.zeros_like(meta)
    meta[0:1, :] = docs_f_ref[...].astype(jnp.float32)
    meta[1:2, :] = docs_b_ref[...].astype(jnp.float32)
    meta[2:3, :] = g1_ref[...].astype(jnp.float32)
    meta[3:4, :] = g2_ref[...].astype(jnp.float32)
    fill = pltpu.make_async_copy(meta, meta_out.at[me.c, me.chip()], local_sems.at[2])
    fill.start()
    meet(weights.partners() + codec.partners())
    codec.begin()
    for copy in fills:
        copy.wait()
    weights.begin()
    fill.wait()

    def meta_column(dx):
        x = lax.rem(me.x + (dx + NX), NX)
        return meta_out.at[me.c, pl.ds(x * NYH, NYH)]

    m_y = []
    for dy in (1, -1, 2):
        ref = meta_out.at[me.c, me.chip()]
        m_y.append((wire.send(ref, ref, me.device(dy=dy)), dy))
    codec.pair(local_sems.at[3])
    for k, dy in m_y:
        wire.arrived(k, meta_out.at[me.c, me.chip(0, -dy)])
    m_x = []
    for dx in (1, -1, 2):
        ref = meta_column(0)
        m_x.append((wire.send(ref, ref, me.device(dx=dx)), dx))
    codec.columns()
    weights.y_near()
    codec.planes()
    for k, dx in m_x:
        wire.arrived(k, meta_column(-dx))
    ref = meta_out.at[me.c]
    m_s = wire.send(ref, ref, me.device(dc=1))
    weights.x_near(0)
    weights.y_far()
    codec.step(1)
    weights.x_near(-1)
    codec.step(2)
    weights.x_near(1)
    codec.step(3)
    weights.x_near(2)
    for dy in (0, -1, 1, 2):
        weights.x_far(dy)
    codec.step(4)
    wire.arrived(m_s, meta_out.at[1 - me.c])
    weights.end()
    codec.end()
    wire.finish()


ANY = pl.BlockSpec(memory_space=pl.ANY)
VMEM = pl.BlockSpec(memory_space=pltpu.VMEM)


def gather_weights(codec, wqkv, wout, docs_f, docs_b, g1, g2):
    copies = 96
    return pl.pallas_call(
        weights_kernel,
        out_shape=(
            jax.ShapeDtypeStruct((D, R), jnp.bfloat16),
            jax.ShapeDtypeStruct((NSEQ, TOK, WCAT), jnp.bfloat16),
            jax.ShapeDtypeStruct((NC, NX * NYH, 8, TOK), jnp.float32),
        ),
        in_specs=[VMEM, ANY, ANY, VMEM, VMEM, VMEM, VMEM],
        out_specs=(ANY, ANY, ANY),
        scratch_shapes=[
            pltpu.VMEM((CROWS, R), jnp.bfloat16),
            pltpu.VMEM((CROWS, R), jnp.bfloat16),
            pltpu.VMEM((CROWS, R), jnp.bfloat16),
            pltpu.VMEM((8, TOK), jnp.float32),
            pltpu.SemaphoreType.DMA((copies,)),
            pltpu.SemaphoreType.DMA((copies,)),
            pltpu.SemaphoreType.DMA((4,)),
        ],
        compiler_params=pltpu.CompilerParams(collective_id=0, has_side_effects=True),
        name="gather_weights",
    )(codec, wqkv, wout, docs_f, docs_b, g1, g2)


def tokens_kernel(own_ref, out, send_sems, recv_sems, local_sem):
    me = Place()
    wire = Wire(send_sems, recv_sems)
    gather = SectionGather(me, wire, out, TOK)
    fill = pltpu.make_async_copy(own_ref, out.at[me.slot()], local_sem)
    fill.start()
    meet(gather.partners())
    fill.wait()
    gather.begin()
    gather.y_near()
    gather.x_near(0)
    gather.y_far()
    gather.x_near(-1)
    gather.x_near(1)
    gather.x_near(2)
    for dy in (0, -1, 1, 2):
        gather.x_far(dy)
    gather.end()
    wire.finish()


def gather_tokens(own):
    copies = 40
    return pl.pallas_call(
        tokens_kernel,
        out_shape=jax.ShapeDtypeStruct((NSEQ,) + own.shape, own.dtype),
        in_specs=[ANY],
        out_specs=ANY,
        scratch_shapes=[
            pltpu.SemaphoreType.DMA((copies,)),
            pltpu.SemaphoreType.DMA((copies,)),
            pltpu.SemaphoreType.DMA,
        ],
        compiler_params=pltpu.CompilerParams(collective_id=1, has_side_effects=True),
        name="gather_tokens",
    )(own)


def add_into(dst, *others):
    total = dst[...].astype(jnp.float32)
    for other in others:
        total = total + other[...].astype(jnp.float32)
    dst[...] = total.astype(dst.dtype)


def scatter_kernel(
    terms, out, pair, part, far_up, far_down, near_up, near_down, row,
    yfar_up, yfar_down, ynear_up, ynear_down, send_sems, recv_sems,
):
    me = Place()
    wire = Wire(send_sems, recv_sems)
    gather = SectionGather(me, wire, None, TOK)
    meet(gather.partners())
    k = wire.send(terms.at[:, 1 - me.c], pair, me.device(dc=1))
    wire.arrived(k, pair)

    @pl.loop(0, NX * NYH)
    def _(i):
        part[i] = (
            terms[i, me.c].astype(jnp.float32) + pair[i].astype(jnp.float32)
        ).astype(jnp.bfloat16)

    def at_x(dx):
        return lax.rem(me.x + (dx + NX), NX) * NYH

    def group(dx, first, count):
        return part.at[pl.ds(at_x(dx) + first, count)]

    half = NYH // 2
    a = wire.send(group(2, 0, half), far_up, me.device(dx=1))
    b = wire.send(group(2, half, half), far_down, me.device(dx=-1))
    c = wire.send(group(1, half, half), near_up.at[pl.ds(half, half)], me.device(dx=1))
    d = wire.send(group(-1, 0, half), near_down.at[pl.ds(0, half)], me.device(dx=-1))
    wire.arrived(a, far_up)
    add_into(group(1, 0, half), far_up)
    e = wire.send(group(1, 0, half), near_up.at[pl.ds(0, half)], me.device(dx=1))
    wire.arrived(b, far_down)
    add_into(group(-1, half, half), far_down)
    f = wire.send(group(-1, half, half), near_down.at[pl.ds(half, half)], me.device(dx=-1))
    wire.arrived(c, near_up.at[pl.ds(half, half)])
    wire.arrived(d, near_down.at[pl.ds(0, half)])
    wire.arrived(e, near_up.at[pl.ds(0, half)])
    wire.arrived(f, near_down.at[pl.ds(half, half)])
    mine = at_x(0)

    @pl.loop(0, NYH)
    def _(i):
        row[i] = (
            part[mine + i].astype(jnp.float32)
            + near_up[i].astype(jnp.float32)
            + near_down[i].astype(jnp.float32)
        ).astype(jnp.bfloat16)

    def at_y(dy):
        return lax.rem(me.yh + (dy + NYH), NYH)

    rows = TOK // 2
    low, high = pl.ds(0, rows), pl.ds(rows, rows)
    a = wire.send(row.at[at_y(2), low], yfar_up, me.device(dy=1))
    b = wire.send(row.at[at_y(2), high], yfar_down, me.device(dy=-1))
    c = wire.send(row.at[at_y(1), high], ynear_up.at[high], me.device(dy=1))
    d = wire.send(row.at[at_y(-1), low], ynear_down.at[low], me.device(dy=-1))
    wire.arrived(a, yfar_up)
    add_into(row.at[at_y(1), low], yfar_up)
    e = wire.send(row.at[at_y(1), low], ynear_up.at[low], me.device(dy=1))
    wire.arrived(b, yfar_down)
    add_into(row.at[at_y(-1), high], yfar_down)
    f = wire.send(row.at[at_y(-1), high], ynear_down.at[high], me.device(dy=-1))
    wire.arrived(c, ynear_up.at[high])
    wire.arrived(d, ynear_down.at[low])
    wire.arrived(e, ynear_up.at[low])
    wire.arrived(f, ynear_down.at[high])
    out[...] = (
        row[at_y(0)].astype(jnp.float32)
        + ynear_up[...].astype(jnp.float32)
        + ynear_down[...].astype(jnp.float32)
    )
    wire.finish()


def scatter_terms(terms):
    copies = 16
    width = terms.shape[-1]
    b16 = jnp.bfloat16
    return pl.pallas_call(
        scatter_kernel,
        out_shape=jax.ShapeDtypeStruct((TOK, width), jnp.float32),
        in_specs=[VMEM],
        out_specs=VMEM,
        scratch_shapes=[
            pltpu.VMEM((NX * NYH, TOK, width), b16),
            pltpu.VMEM((NX * NYH, TOK, width), b16),
            pltpu.VMEM((NYH // 2, TOK, width), b16),
            pltpu.VMEM((NYH // 2, TOK, width), b16),
            pltpu.VMEM((NYH, TOK, width), b16),
            pltpu.VMEM((NYH, TOK, width), b16),
            pltpu.VMEM((NYH, TOK, width), b16),
            pltpu.VMEM((TOK // 2, width), b16),
            pltpu.VMEM((TOK // 2, width), b16),
            pltpu.VMEM((TOK, width), b16),
            pltpu.VMEM((TOK, width), b16),
            pltpu.SemaphoreType.DMA((copies,)),
            pltpu.SemaphoreType.DMA((copies,)),
        ],
        compiler_params=pltpu.CompilerParams(
            collective_id=2, has_side_effects=True, vmem_limit_bytes=32 * 2**20
        ),
        name="scatter_terms",
    )(terms.reshape(NX * NYH, NC, TOK, width))


def shifted(value, axis, steps):
    count = lax.axis_size(axis)
    pairs = [(source, (source + steps) % count) for source in range(count)]
    return lax.ppermute(value, axis, pairs)


def rms_factor(values):
    return lax.rsqrt(jnp.mean(values * values, axis=-1, keepdims=True) + EPS)


def to_heads(matrix, rows):
    return matrix.reshape(rows, HQ, HD).transpose(1, 0, 2)


def from_heads(heads, rows):
    return heads.transpose(1, 0, 2).reshape(rows, HQ * HD)


def on_device(
    codes_fwd, saved_stream, grad_codes, docs_fwd, docs_bwd, codec, wqkv, wout, gain_attn, gain_code
):
    rows = codes_fwd.shape[1]
    scale = HD ** (-0.5)
    enc_scale = (R / D) ** 0.5
    codec_all, w_cat, meta = gather_weights(
        codec, wqkv, wout, docs_fwd, docs_bwd, gain_attn, gain_code
    )
    w_cat = w_cat.reshape(D, WCAT)
    w_all, o_all = w_cat[:, :QKV], w_cat[:, QKV:]
    meta = meta.transpose(2, 1, 0, 3).reshape(8, D)
    all_docs_f, all_docs_b = meta[0:1], meta[1:2]
    g_attn, g_code = meta[2:3], meta[3:4]
    place = lax.axis_index("seq") * rows + jnp.arange(rows, dtype=jnp.int32)
    k_pos = jnp.arange(D, dtype=jnp.int32)
    causal = k_pos[None, :] <= place[:, None]
    contract_last = (((1,), (1,)), ((), ()))

    def project(stream):
        scale1 = rms_factor(stream)
        normed = (stream * scale1 * g_attn).astype(jnp.bfloat16)
        return scale1, jnp.dot(normed, w_all, preferred_element_type=jnp.float32).astype(
            jnp.bfloat16
        )

    def finish_forward(stream, attended):
        return stream + lax.dot_general(
            attended, o_all, contract_last, preferred_element_type=jnp.float32
        )

    def attend(queries, keys, values, docs, all_docs):
        allowed = (causal & (all_docs == docs.astype(jnp.float32)[:, None]))[None]
        scores = (
            jnp.einsum("htd,sd->hts", queries, keys, preferred_element_type=jnp.float32) * scale
        )
        masked = jnp.where(allowed, scores, -1e30)
        top = jnp.max(masked, axis=-1, keepdims=True)
        probs = jnp.where(allowed, jnp.exp(masked - top), 0.0)
        denom = jnp.sum(probs, axis=-1, keepdims=True)
        summed = jnp.einsum(
            "hts,sd->htd", probs.astype(jnp.bfloat16), values, preferred_element_type=jnp.float32
        )
        return probs, denom, (summed / denom).astype(jnp.bfloat16)

    stream = lax.dot_general(
        codes_fwd[0], codec_all, contract_last, preferred_element_type=jnp.float32
    )
    _, qkv = project(stream)
    saved = saved_stream[0].astype(jnp.float32)
    scale1, qkv_b = project(saved)
    kv = gather_tokens(jnp.concatenate([qkv[:, QW:], qkv_b[:, QW:]], axis=1)).reshape(D, QKV)

    _, _, heads = attend(
        to_heads(qkv[:, :QW], rows), kv[:, :HD], kv[:, HD : 2 * HD], docs_fwd[0], all_docs_f
    )
    mixed = finish_forward(stream, from_heads(heads, rows))
    normed = (mixed * rms_factor(mixed) * g_code).astype(jnp.bfloat16)
    coded = (jnp.dot(normed, codec_all, preferred_element_type=jnp.float32) * enc_scale).astype(
        jnp.bfloat16
    )
    codes_out = shifted(coded, "section", 1)

    stream = saved
    queries_b = to_heads(qkv_b[:, :QW], rows)
    all_keys, all_values = kv[:, 2 * HD : 3 * HD], kv[:, 3 * HD :]
    probs, denom, attended_heads = attend(
        queries_b, all_keys, all_values, docs_bwd[0], all_docs_b
    )
    mixed = finish_forward(stream, from_heads(attended_heads, rows))
    scale2 = rms_factor(mixed)
    pre2 = mixed * scale2
    grad_n2 = (
        lax.dot_general(grad_codes[0], codec_all, contract_last, preferred_element_type=jnp.float32)
        * enc_scale
    )
    weighted2 = grad_n2 * g_code
    grad_mixed = scale2 * (weighted2 - pre2 * jnp.mean(weighted2 * pre2, axis=-1, keepdims=True))
    grad_att = jnp.dot(
        grad_mixed.astype(jnp.bfloat16), o_all, preferred_element_type=jnp.float32
    ).astype(jnp.bfloat16)
    grad_heads = to_heads(grad_att, rows)
    grad_p = jnp.einsum("htd,sd->hts", grad_heads, all_values, preferred_element_type=jnp.float32)
    delta = jnp.einsum(
        "htd,htd->ht", grad_heads.astype(jnp.float32), attended_heads.astype(jnp.float32)
    )
    grad_s = (probs / denom * (grad_p - delta[..., None]) * scale).astype(jnp.bfloat16)
    probs_b = (probs / denom).astype(jnp.bfloat16)
    grad_q = from_heads(
        jnp.einsum("hts,sd->htd", grad_s, all_keys, preferred_element_type=jnp.float32), rows
    )
    key_term = jnp.einsum("hts,htd->sd", grad_s, queries_b, preferred_element_type=jnp.float32)
    value_term = jnp.einsum("hts,htd->sd", probs_b, grad_heads, preferred_element_type=jnp.float32)
    kv_grad = scatter_terms(
        jnp.concatenate([key_term, value_term], axis=1).astype(jnp.bfloat16)
    )
    grad_qkv = jnp.concatenate([grad_q, kv_grad], axis=1).astype(jnp.bfloat16)
    grad_n1 = lax.dot_general(grad_qkv, w_all, contract_last, preferred_element_type=jnp.float32)
    pre1 = stream * scale1
    weighted1 = grad_n1 * g_attn
    grad_stream = grad_mixed + scale1 * (
        weighted1 - pre1 * jnp.mean(weighted1 * pre1, axis=-1, keepdims=True)
    )
    grad_in = jnp.dot(
        grad_stream.astype(jnp.bfloat16), codec_all, preferred_element_type=jnp.float32
    ).astype(jnp.bfloat16)
    grads_out = shifted(grad_in, "section", -1)
    return (codes_out[None], grads_out[None])


def solution(mesh):
    return jax.shard_map(
        on_device,
        mesh=mesh,
        in_specs=(
            P("section", "seq", None),
            P("section", "seq", None),
            P("section", "seq", None),
            P("section", "seq"),
            P("section", "seq"),
            P(("section", "seq"), None),
            P("section", "seq", None),
            P("section", "seq", None),
            P("section", "seq"),
            P("section", "seq"),
        ),
        out_specs=(P("section", "seq", None), P("section", "seq", None)),
        check_vma=False,
    )
```

time: 1310 us -> 202 us (0.15)
  waiting for transfers between devices: 1040 us -> 1.92 us
  blocking collectives: 173 us -> 0 us
  Pallas kernels: 0 us -> 125 us
  between operations: 14.6 us -> 1.14 us
    all_gather x7 -> x0, waiting for transfers between devices: 949 us -> none  [the longest x1 796 us: on_device(): codec_all = lax.all_gather(codec, ('section', 'seq'), axis=0, tiled=True)]
    all_gather x4 -> x0, blocking collectives: 173 us -> none  [the longest x1 46.5 us: on_device(): lax.all_gather(gain_attn, 'seq', axis=1, tiled=True)]
    pallas_call x0 -> x3, Pallas kernels: none -> 125 us  [the longest x1 68 us: gather_weights(): pl.pallas_call(weights_kernel, out_shape=(jax.ShapeDtypeStruct((D, R), jn...]
    unnamed x9 -> x0, waiting for transfers between devices: 91.1 us -> none
  transfers between devices with their start and end apart: 10 -> 2, of which waited for: 7 -> 1; matrix products, arithmetic and copies ran while one was open for 5% -> 17% of each run, Pallas kernels for 0% -> 12%
where the time goes in v1:
time: 202 us; the launch traced here: 199 us
  Pallas kernels  125 us (62%)
  matrix products  49.2 us (24%)
  starting transfers between devices  7.7 us (4%)
  local copies, waits for them, and re-layouts  7.64 us (4%)
  other arithmetic  6.35 us (3%)
    pallas_call x1, Pallas kernels, gather_weights(): pl.pallas_call(weights_kernel, out_shape=(jax.ShapeDtypeStruct((D, R), jn...  68 us
    pallas_call x1, Pallas kernels, gather_tokens(): pl.pallas_call(tokens_kernel, out_shape=jax.ShapeDtypeStruct((NSEQ,) + ow...  33.3 us
    pallas_call x1, Pallas kernels, scatter_terms(): pl.pallas_call(scatter_kernel, out_shape=jax.ShapeDtypeStruct((TOK, width...  23.7 us
    sub x2, matrix products, attend(): probs = jnp.where(allowed, jnp.exp(masked - top), 0.0)  9.01 us
    dot_general x2, matrix products, attend(): jnp.einsum('hts,sd->htd', probs.astype(jnp.bfloat16), values, preferred_e...  7.9 us
    ppermute x2, starting transfers between devices, shifted(): return lax.ppermute(value, axis, pairs)  7.7 us
    unnamed x49, local copies, waits for them, and re-layouts  6.31 us
    dot_general x2, matrix products, finish_forward(): lax.dot_general(attended, o_all, contract_last, preferred_element_type=jn...  5.66 us
  transfers between devices with their start and end apart: 2, of which 1 were waited for; matrix products, arithmetic and copies ran while one was open for 17% of the time, Pallas kernels for 12%

profile of v1, /device:TPU:1, one launch (start us, length us, event | category | flops | bytes accessed | tf_op | source)
XLA Modules:
  0.0 199.0 jit_solution(1678044815807999342)
XLA Ops:
  0.7 1.6 copy.28
  2.9 68.0 %gather_weights.1 = (bf16[4096,512]{1,0:T(8,128)(2,1)}, bf16[32,128,768]{2,1,0:T(8,128)(2,1)}, f32[2,16,8,128]{3,2,1,0:T(8,128)}) custom-call(bf16[8,512]{1,0:T(8,128)(2,1)} %codec_ref.1, bf16[1,128,512]{2,1,0:T(8,128)(2,1)} %wqkv_ref.1, bf16[1,128,256]{2,1,0:T(8,128)(2,1)} %wout_ref.1, s32[1,128]{1,0:T(1,128)} %docs_f_ref.1, s32[1,128]{1,0:T(1,128)} %docs_b_ref.1, ...), custom_call_target="tpu_custom_call" | custom-call | tf_op jit(solution)/shard_map/gather_weights/pallas_call | solution.py:350
  72.2 3.6 %multiply_reduce_fusion.3 = (f32[128]{0:T(128)S(1)}, f32[128,4096]{0,1:T(8,128)S(1)}) fusion(bf16[4096,512]{1,0:T(8,128)(2,1)} %get-tuple-element.5, bf16[1,128,512]{2,1,0:T(8,128)(2,1)S(1)} %copy-done), kind=kOutput, calls=%fused_computation.56 | convolution fusion | flops 537919360 | bytes 6423040 | tf_op jit(solution)/shard_map/dot_general | solution.py:587
  80.1 33.3 %gather_tokens.1 = bf16[32,128,512]{2,1,0:T(8,128)(2,1)} custom-call(bf16[128,512]{1,0:T(8,128)(2,1)} %pad_maximum_fusion.1.own_ref), custom_call_target="tpu_custom_call" | custom-call | tf_op jit(solution)/shard_map/gather_tokens/pallas_call | solution.py:396
  113.4 1.9 fusion.36
  115.3 3.7 %fusion.103 = f32[2,128]{1,0:T(2,128)S(1)} fusion(pred[128,4096]{1,0:T(8,128)(4,1)} %get-tuple-element.17, bf16[4096,512]{1,0:T(8,128)(2,1)} %bitcast.179, bf16[16,2,8,128]{3,2,1,0:T(8,128)(2,1)S(1)} %get-tuple-element.33), kind=kOutput, calls=%fused_computation.133 | convolution fusion | flops 273682432 | bytes 2163712 | tf_op jit(solution)/shard_map/sub | solution.py:580
  119.0 4.6 %fusion.58 = bf16[128,2,128]{0,2,1:T(8,128)(2,1)S(1)} fusion(bf16[4096,512]{1,0:T(8,128)(2,1)} %bitcast.180, f32[128,2]{0,1:T(2,128)S(1)} %bitcast.200, pred[128,4096]{1,0:T(8,128)(4,1)} %get-tuple-element.17, bf16[16,2,8,128]{3,2,1,0:T(8,128)(2,1)S(1)} %get-tuple-element.33), kind=kOutput, calls=%fused_computation.73 | convolution fusion | flops 542183680 | bytes 3277824 | tf_op jit(solution)/shard_map/hts,sd->htd/dot_general | solution.py:582
  123.6 2.9 %multiply_reduce_fusion.2 = (f32[128]{0:T(128)S(1)}, f32[128,4096]{0,1:T(8,128)S(1)}) fusion(f32[128,4096]{0,1:T(8,128)S(1)} %get-tuple-element.19, bf16[128,256]{0,1:T(8,128)(2,1)S(1)} %bitcast.192, bf16[4096,768]{1,0:T(8,128)(2,1)} %bitcast.173), kind=kOutput, calls=%fused_computation.52 | convolution fusion | flops 270008192 | bytes 6357504 | tf_op jit(solution)/shard_map/dot_general | solution.py:569
  126.6 2.2 %fusion.48 = bf16[128,512]{1,0:T(8,128)(2,1)} fusion(bf16[4096,512]{1,0:T(8,128)(2,1)S(1)} %copy-done.1, f32[128,4096]{0,1:T(8,128)S(1)} %get-tuple-element.21, f32[4096]{0:T(1024)S(1)} %bitcast.189, f32[128]{0:T(128)S(1)} %add_rsqrt_fusion.1), kind=kOutput, calls=%fused_computation.68 | convolution fusion | flops 538574848 | bytes 6439424 | tf_op jit(solution)/shard_map/dot_general | solution.py:600
  128.8 3.0 %collective-permute-start = (bf16[128,512]{1,0:T(8,128)(2,1)}, bf16[128,512]{1,0:T(8,128)(2,1)}, u32[]{:S(2)}, u32[]{:S(2)}) collective-permute-start(bf16[128,512]{1,0:T(8,128)(2,1)} %fusion.48), channel_id=1, source_target_pairs={{0,32},{32,64},{64,96},{96,128},{128,160},{160,192},{192,224},{224... | collective-permute-start | bytes 393224 | tf_op jit(solution)/shard_map/ppermute | solution.py:527
  131.8 5.3 %fusion.104 = (f32[2,128]{1,0:T(2,128)S(1)}, f32[2,128,4096]{2,1,0:T(8,128)}) fusion(pred[128,4096]{1,0:T(8,128)(4,1)S(1)} %copy-done.8, bf16[4096,512]{1,0:T(8,128)(2,1)} %bitcast.181, bf16[16,2,8,128]{3,2,1,0:T(8,128)(2,1)S(1)} %get-tuple-element.8), kind=kOutput, calls=%fused_computation.134 | convolution fusion | flops 273682432 | bytes 6358016 | tf_op jit(solution)/shard_map/sub | solution.py:580
  137.1 3.3 %fusion.81 = (bf16[128,2,128]{0,2,1:T(8,128)(2,1)S(1)}, f32[2,128,128]{1,2,0:T(8,128)S(1)}) fusion(f32[128,2]{0,1:T(2,128)S(1)} %bitcast.199, bf16[4096,512]{1,0:T(8,128)(2,1)} %bitcast.182, f32[2,128,4096]{2,1,0:T(8,128)} %get-tuple-element.23), kind=kOutput, calls=%fused_computation.96 | convolution fusion | flops 269549568 | bytes 5440512 | tf_op jit(solution)/shard_map/hts,sd->htd/dot_general | solution.py:582
  140.5 2.7 %multiply_reduce_fusion.1 = (f32[128]{0:T(128)S(1)}, f32[128,4096]{0,1:T(8,128)S(1)}) fusion(bf16[128,256]{0,1:T(8,128)(2,1)S(1)} %bitcast.187, bf16[4096,768]{1,0:T(8,128)(2,1)} %bitcast.174, bf16[1,128,4096]{1,2,0:T(8,128)(2,1)S(1)} %copy.28), kind=kOutput, calls=%fused_computation.48 | convolution fusion | flops 270532480 | bytes 5308928 | tf_op jit(solution)/shard_map/dot_general | solution.py:569
  144.6 3.1 %fusion.61 = bf16[16,2,8,128]{3,2,1,0:T(8,128)(2,1)S(1)} fusion(bf16[4096,768]{1,0:T(8,128)(2,1)} %bitcast.175, f32[128,4096]{0,1:T(8,128)S(1)} %get-tuple-element.29, f32[128,4096]{0,1:T(8,128)S(1)} %get-tuple-element.27, f32[128]{0:T(128)S(1)} %broadcast_multiply_fusion.2, f32[128]{0:T(128)S(1)} %add_rsqrt_fusion), kind=kOutput, calls=%fused_computation.74 | convolution fusion | flops 271089664 | bytes 6358016 | tf_op jit(solution)/shard_map/dot_general | solution.py:620
  148.5 1.8 fusion.15
  152.0 3.3 %fusion.12 = bf16[2,128,4096]{2,1,0:T(8,128)(2,1)S(1)} fusion(f32[2,128]{1,0:T(2,128)S(1)} %multiply_reduce_fusion.4, f32[2,128,4096]{2,1,0:T(8,128)} %get-tuple-element.23, f32[2,128]{1,0:T(2,128)} %copy-done.15, bf16[4096,512]{1,0:T(8,128)(2,1)} %bitcast.183, bf16[16,2,8,128]{3,2,1,0:T(8,128)(2,1)} %copy-done.9), kind=kOutput, calls=%fused_computation.15 | convolution fusion | flops 273678336 | bytes 7407616 | tf_op jit(solution)/shard_map/htd,sd->hts/dot_general | solution.py:624
  155.3 2.1 %convolution_convert_fusion.1 = bf16[2,128,128]{1,2,0:T(8,128)(2,1)S(1)} fusion(bf16[2,128,4096]{2,1,0:T(8,128)(2,1)S(1)} %fusion.12, bf16[4096,512]{1,0:T(8,128)(2,1)} %bitcast.184), kind=kOutput, calls=%fused_computation.72 | convolution fusion | flops 268468224 | bytes 3211264 | tf_op jit(solution)/shard_map/hts,sd->htd/dot_general | solution.py:631
  157.5 1.7 fusion.14
  159.3 1.8 pad_maximum_fusion.terms
  161.2 23.7 %scatter_terms.1 = f32[128,256]{1,0:T(8,128)S(1)} custom-call(bf16[16,2,128,256]{3,2,1,0:T(8,128)(2,1)S(1)} %pad_maximum_fusion.terms), custom_call_target="tpu_custom_call" | custom-call | tf_op jit(solution)/shard_map/scatter_terms/pallas_call | solution.py:497
  184.9 3.2 %fusion.25 = (f32[128]{0:T(128)S(1)}, f32[128,4096]{0,1:T(8,128)S(1)}) fusion(bf16[1,128,4096]{1,2,0:T(8,128)(2,1)S(1)} %copy.28, f32[128]{0:T(128)S(1)} %copy-done.21, f32[4096]{0:T(1024)S(1)} %bitcast.195, bf16[4096,768]{1,0:T(8,128)(2,1)} %bitcast.176, bf16[128,256]{1,0:T(8,128)(2,1)S(1)} %convert.20, bf16[128,256]{1,0:T(8,128)(2,1)S(1)} %copy.57), kind=kOutput, calls=%fused_computation.37 | convolution fusion | flops 539754368 | bytes 7488512 | tf_op jit(solution)/shard_map/dot_general | solution.py:639
  190.2 4.7 %collective-permute-start.1 = (bf16[128,512]{1,0:T(8,128)(2,1)S(1)}, bf16[128,512]{1,0:T(8,128)(2,1)S(1)}, u32[]{:S(2)}, u32[]{:S(2)}) collective-permute-start(bf16[128,512]{1,0:T(8,128)(2,1)S(1)} %convolution_convert_fusion), channel_id=1, source_target_pairs={{0,480},{32,0},{64,32},{96,64},{128,96},{160,128},{192,160},{224,1... | collective-permute-start | bytes 393224 | tf_op jit(solution)/shard_map/ppermute | solution.py:527
  194.8 1.9 collective-permute-done.1
  196.8 1.6 copy.100
  (72 shorter events, 12.6 us)
Async XLA Ops:
  0.6 71.6 %copy-start = (bf16[1,128,512]{2,1,0:T(8,128)(2,1)S(1)}, bf16[1,128,512]{2,1,0:T(8,128)(2,1)}, u32[]{:S(2)}) copy-start(bf16[1,128,512]{2,1,0:T(8,128)(2,1)} %param.10) | copy-start | bytes 393220
  0.6 2.3 %copy-start.17 = (s32[1,128]{1,0:T(1,128)S(1)}, s32[1,128]{1,0:T(1,128)}, u32[]{:S(2)}) copy-start(s32[1,128]{1,0:T(1,128)} %docs_b_ref.1) | copy-start | bytes 1540
  0.7 2.3 %copy-start.16 = (s32[1,128]{1,0:T(1,128)S(1)}, s32[1,128]{1,0:T(1,128)}, u32[]{:S(2)}) copy-start(s32[1,128]{1,0:T(1,128)} %docs_f_ref.1) | copy-start | bytes 1540
  2.9 72.9 %copy-start.20 = (f32[128]{0:T(128)}, f32[128]{0:T(128)S(1)}, u32[]{:S(2)}) copy-start(f32[128]{0:T(128)S(1)} %add_rsqrt_fusion.2) | copy-start | bytes 1540
  72.2 4.0 %copy-start.6 = (bf16[32,128,768]{2,1,0:T(8,128)(2,1)S(1)}, bf16[32,128,768]{2,1,0:T(8,128)(2,1)}, u32[]{:S(2)}) copy-start(bf16[32,128,768]{2,1,0:T(8,128)(2,1)} %get-tuple-element.7) | copy-start | bytes 18874372
  79.4 52.4 %copy-start.10 = (bf16[16,2,8,128]{3,2,1,0:T(8,128)(2,1)}, bf16[16,2,8,128]{3,2,1,0:T(8,128)(2,1)S(1)}, u32[]{:S(2)}) copy-start(bf16[16,2,8,128]{3,2,1,0:T(8,128)(2,1)S(1)} %get-tuple-element.8) | copy-start | bytes 196612
  123.6 3.0 %copy-start.1 = (bf16[4096,512]{1,0:T(8,128)(2,1)S(1)}, bf16[4096,512]{1,0:T(8,128)(2,1)}, u32[]{:S(2)}) copy-start(bf16[4096,512]{1,0:T(8,128)(2,1)} %get-tuple-element.5) | copy-start | bytes 12582916
  126.6 5.3 %copy-start.8 = (pred[128,4096]{1,0:T(8,128)(4,1)S(1)}, pred[128,4096]{1,0:T(8,128)(4,1)}, u32[]{:S(2)}) copy-start(pred[128,4096]{1,0:T(8,128)(4,1)} %get-tuple-element.16) | copy-start | bytes 1572868
  128.8 66.1 %collective-permute-start = (bf16[128,512]{1,0:T(8,128)(2,1)}, bf16[128,512]{1,0:T(8,128)(2,1)}, u32[]{:S(2)}, u32[]{:S(2)}) collective-permute-start(bf16[128,512]{1,0:T(8,128)(2,1)} %fusion.48), channel_id=1, source_target_pairs={{0,32},{32,64},{64,96},{96,128},{128,160},{160,192},{192,224},{224... | collective-permute-start | bytes 393224 | tf_op jit(solution)/shard_map/ppermute | solution.py:527
  137.1 11.3 %copy-start.15 = (f32[2,128]{1,0:T(2,128)}, f32[2,128]{1,0:T(2,128)S(1)}, u32[]{:S(2)}) copy-start(f32[2,128]{1,0:T(2,128)S(1)} %get-tuple-element.22) | copy-start | bytes 3076
  140.5 2.8 %copy-start.2 = (bf16[4096,512]{1,0:T(8,128)(2,1)S(1)}, bf16[4096,512]{1,0:T(8,128)(2,1)}, u32[]{:S(2)}) copy-start(bf16[4096,512]{1,0:T(8,128)(2,1)} %get-tuple-element.5) | copy-start | bytes 12582916
  140.5 2.8 %copy-start.12 = (bf16[1,128,512]{2,1,0:T(8,128)(2,1)S(1)}, bf16[1,128,512]{2,1,0:T(8,128)(2,1)}, u32[]{:S(2)}) copy-start(bf16[1,128,512]{2,1,0:T(8,128)(2,1)} %param.12) | copy-start | bytes 393220
  143.2 1.4 copy-start.13
  144.6 3.2 %copy-start.4 = (f32[128,4096]{0,1:T(8,128)}, f32[128,4096]{0,1:T(8,128)S(1)}, u32[]{:S(2)}) copy-start(f32[128,4096]{0,1:T(8,128)S(1)} %get-tuple-element.29) | copy-start | bytes 6291460
  144.6 3.2 %copy-start.18 = (f32[128]{0:T(128)}, f32[128]{0:T(128)S(1)}, u32[]{:S(2)}) copy-start(f32[128]{0:T(128)S(1)} %broadcast_multiply_fusion.2) | copy-start | bytes 1540
  144.6 3.8 %copy-start.7 = (f32[2,128,4096]{2,1,0:T(8,128)S(1)}, f32[2,128,4096]{2,1,0:T(8,128)}, u32[]{:S(2)}) copy-start(f32[2,128,4096]{2,1,0:T(8,128)} %get-tuple-element.23) | copy-start | bytes 12582916
  147.8 0.7 copy-start.9
  155.3 2.1 %copy-start.11 = (bf16[16,2,8,128]{3,2,1,0:T(8,128)(2,1)S(1)}, bf16[16,2,8,128]{3,2,1,0:T(8,128)(2,1)}, u32[]{:S(2)}) copy-start(bf16[16,2,8,128]{3,2,1,0:T(8,128)(2,1)} %copy-done.10) | copy-start | bytes 196612
  161.1 23.7 %copy-start.21 = (f32[128]{0:T(128)S(1)}, f32[128]{0:T(128)}, u32[]{:S(2)}) copy-start(f32[128]{0:T(128)} %copy-done.20) | copy-start | bytes 1540
  184.9 3.5 %copy-start.3 = (bf16[4096,512]{1,0:T(8,128)(2,1)S(1)}, bf16[4096,512]{1,0:T(8,128)(2,1)}, u32[]{:S(2)}) copy-start(bf16[4096,512]{1,0:T(8,128)(2,1)} %get-tuple-element.5) | copy-start | bytes 12582916
  184.9 4.1 %copy-start.5 = (f32[128,4096]{0,1:T(8,128)S(1)}, f32[128,4096]{0,1:T(8,128)}, u32[]{:S(2)}) copy-start(f32[128,4096]{0,1:T(8,128)} %copy-done.4) | copy-start | bytes 6291460
  184.9 4.1 %copy-start.14 = (f32[128]{0:T(128)S(1)}, f32[128]{0:T(128)}, u32[]{:S(2)}) copy-start(f32[128]{0:T(128)} %copy-done.13) | copy-start | bytes 1540
  184.9 4.1 %copy-start.19 = (f32[128]{0:T(128)S(1)}, f32[128]{0:T(128)}, u32[]{:S(2)}) copy-start(f32[128]{0:T(128)} %copy-done.18) | copy-start | bytes 1540
  190.2 6.6 %collective-permute-start.1 = (bf16[128,512]{1,0:T(8,128)(2,1)S(1)}, bf16[128,512]{1,0:T(8,128)(2,1)S(1)}, u32[]{:S(2)}, u32[]{:S(2)}) collective-permute-start(bf16[128,512]{1,0:T(8,128)(2,1)S(1)} %convolution_convert_fusion), channel_id=1, source_target_pairs={{0,480},{32,0},{64,32},{96,64},{128,96},{160,128},{192,160},{224,1... | collective-permute-start | bytes 393224 | tf_op jit(solution)/shard_map/ppermute | solution.py:527

commit v2 on v1

v2 whole, which is shorter than its diff:
```python
import functools

import jax
import jax.numpy as jnp
from jax import lax
from jax.experimental import pallas as pl
from jax.experimental.pallas import tpu as pltpu
from jax.sharding import PartitionSpec as P

D = 4096
R = 512
HD = 128
HQ = 2
TOK = 128
QKV = (HQ + 2) * HD
QW = HQ * HD
NX, NYH, NC = 4, 4, 2
NYL, NZ = 2, 8
NSEQ = NX * NYH * NC
NG = NX
GW = D // NG
GS = NSEQ // NG
KEYS = 512
KS = KEYS // TOK
NK = D // KEYS

EPS = 1e-05


class Place:
    def __init__(self):
        self.section = lax.axis_index("section")
        self.seq = lax.axis_index("seq")
        self.ylo = self.section // NZ
        self.z = lax.rem(self.section, NZ)
        self.x = self.seq // (NYH * NC)
        self.yh = lax.rem(self.seq // NC, NYH)
        self.c = lax.rem(self.seq, NC)

    def slot(self, dx=0, dy=0, dc=0):
        x = lax.rem(self.x + (dx + NX), NX)
        yh = lax.rem(self.yh + (dy + NYH), NYH)
        c = lax.rem(self.c + dc, NC)
        return (x * NYH + yh) * NC + c

    def chip(self, dx=0, dy=0):
        return lax.rem(self.x + (dx + NX), NX) * NYH + lax.rem(self.yh + (dy + NYH), NYH)

    def device(self, dx=0, dy=0, dc=0, dz=0, dyl=0):
        z = lax.rem(self.z + (dz + NZ), NZ)
        ylo = lax.rem(self.ylo + dyl, NYL)
        return {"section": ylo * NZ + z, "seq": self.slot(dx, dy, dc)}


class Wire:
    def __init__(self, send_sems, recv_sems):
        self.send_sems, self.recv_sems = send_sems, recv_sems
        self.started = []

    def send(self, src, dst, device):
        k = len(self.started)
        copy = pltpu.make_async_remote_copy(
            src_ref=src,
            dst_ref=dst,
            send_sem=self.send_sems.at[k],
            recv_sem=self.recv_sems.at[k],
            device_id=device,
            device_id_type=pl.DeviceIdType.MESH,
        )
        copy.start()
        self.started.append(copy)
        return k

    def arrived(self, k, dst):
        pltpu.make_async_copy(dst, dst, self.recv_sems.at[k]).wait()

    def finish(self):
        for copy in self.started:
            copy.wait_send()


def meet(devices):
    barrier = pltpu.get_barrier_semaphore()
    for device in devices:
        pl.semaphore_signal(barrier, inc=1, device_id=device, device_id_type=pl.DeviceIdType.MESH)
    pl.semaphore_wait(barrier, len(devices))


class SectionGather:
    def __init__(self, me, wire, out, rows):
        self.me, self.wire, self.out = me, wire, out
        self.half = rows // 2
        self.sib = []
        self.keys = {}

    def block(self, dx, dy):
        return self.out.at[self.me.slot(dx, dy)]

    def part(self, dx, dy, which):
        return self.out.at[self.me.slot(dx, dy), pl.ds(which * self.half, self.half)]

    def to_sibling(self, dx, dy):
        ref = self.block(dx, dy)
        k = self.wire.send(ref, ref, self.me.device(dc=1))
        self.sib.append((k, dx, dy))

    def begin(self):
        own = self.block(0, 0)
        self.keys["y+"] = self.wire.send(own, own, self.me.device(dy=1))
        self.keys["y-"] = self.wire.send(own, own, self.me.device(dy=-1))
        self.along_x(0)
        self.to_sibling(0, 0)

    def along_x(self, dy):
        ref = self.block(0, dy)
        self.keys["x+", dy] = self.wire.send(ref, ref, self.me.device(dx=1))
        self.keys["x-", dy] = self.wire.send(ref, ref, self.me.device(dx=-1))

    def y_near(self):
        self.wire.arrived(self.keys["y+"], self.block(0, -1))
        ref = self.part(0, -1, 0)
        self.keys["y++"] = self.wire.send(ref, ref, self.me.device(dy=1))
        self.along_x(-1)
        self.wire.arrived(self.keys["y-"], self.block(0, 1))
        ref = self.part(0, 1, 1)
        self.keys["y--"] = self.wire.send(ref, ref, self.me.device(dy=-1))
        self.along_x(1)
        self.to_sibling(0, -1)
        self.to_sibling(0, 1)

    def y_far(self):
        self.wire.arrived(self.keys["y++"], self.part(0, 2, 0))
        self.wire.arrived(self.keys["y--"], self.part(0, 2, 1))
        self.along_x(2)
        self.to_sibling(0, 2)

    def x_near(self, dy):
        self.wire.arrived(self.keys["x+", dy], self.block(-1, dy))
        ref = self.part(-1, dy, 0)
        self.keys["x++", dy] = self.wire.send(ref, ref, self.me.device(dx=1))
        self.wire.arrived(self.keys["x-", dy], self.block(1, dy))
        ref = self.part(1, dy, 1)
        self.keys["x--", dy] = self.wire.send(ref, ref, self.me.device(dx=-1))
        self.to_sibling(-1, dy)
        self.to_sibling(1, dy)

    def x_far(self, dy):
        self.wire.arrived(self.keys["x++", dy], self.part(2, dy, 0))
        self.wire.arrived(self.keys["x--", dy], self.part(2, dy, 1))
        self.to_sibling(2, dy)

    def end(self):
        for k, dx, dy in self.sib:
            self.wire.arrived(k, self.out.at[self.me.slot(dx, dy, 1)])

    def partners(self):
        me = self.me
        return [
            me.device(dy=1),
            me.device(dy=-1),
            me.device(dx=1),
            me.device(dx=-1),
            me.device(dc=1),
        ]


CROWS = 16
PLANE = NX * NYH * CROWS
LANES = R // NC


class CodecGather:
    def __init__(self, me, wire, out, both, other, tile):
        self.me, self.wire, self.out = me, wire, out
        self.both, self.other, self.tile = both, other, tile

    def ref(self, first, rows, dc=0):
        c = lax.rem(self.me.c + dc, NC)
        return self.out.at[
            pl.ds(pl.multiple_of(first, CROWS), rows),
            pl.ds(pl.multiple_of(c * LANES, LANES), LANES),
        ]

    def plane_first(self, dyl, dz):
        me = self.me
        ylo = lax.rem(me.ylo + dyl, NYL)
        return (ylo * NZ + lax.rem(me.z + (dz + NZ), NZ)) * PLANE

    def tile_ref(self, dyl, dy):
        return self.ref(self.plane_first(dyl, 0) + self.me.chip(0, dy) * CROWS, CROWS)

    def column_ref(self, dyl, dx):
        x = lax.rem(self.me.x + (dx + NX), NX)
        return self.ref(self.plane_first(dyl, 0) + x * (NYH * CROWS), NYH * CROWS)

    def plane_ref(self, dyl, dz, dc=0):
        return self.ref(self.plane_first(dyl, dz), PLANE, dc)

    def begin(self):
        self.k_pair = self.wire.send(self.both, self.other, self.me.device(dc=1))

    def pair(self, local_sem):
        me = self.me
        self.wire.arrived(self.k_pair, self.other)
        row = lax.broadcasted_iota(jnp.int32, (CROWS, R), 0)
        mine = (row // (CROWS // NC)) == me.c
        self.tile[...] = jnp.where(
            mine, self.both[...].astype(jnp.float32), self.other[...].astype(jnp.float32)
        ).astype(jnp.bfloat16)
        src = self.tile.at[:, pl.ds(pl.multiple_of(me.c * LANES, LANES), LANES)]
        self.local = pltpu.make_async_copy(src, self.tile_ref(0, 0), local_sem)
        self.local.start()
        self.k_y = []
        for dyl in range(NYL):
            for dy in range(NYH):
                if dyl or dy:
                    k = self.wire.send(src, self.tile_ref(0, 0), me.device(dy=dy, dyl=dyl))
                    self.k_y.append((k, dyl, dy))

    def columns(self):
        me = self.me
        self.local.wait()
        for k, dyl, dy in self.k_y:
            self.wire.arrived(k, self.tile_ref(dyl, -dy))
        self.k_x = []
        for dx in (1, -1, 2):
            for dyl in range(NYL):
                ref = self.column_ref(dyl, 0)
                self.k_x.append((self.wire.send(ref, ref, me.device(dx=dx)), dyl, dx))

    def planes(self):
        for k, dyl, dx in self.k_x:
            self.wire.arrived(k, self.column_ref(dyl, -dx))
        self.k_up, self.k_down, self.sib = {}, {}, []
        for dyl in range(NYL):
            self.pass_on(dyl, 0)

    def pass_on(self, dyl, step):
        me = self.me
        below, above = self.plane_ref(dyl, -step), self.plane_ref(dyl, step)
        if step < NZ // 2 - 1 or (step == NZ // 2 - 1 and dyl == 0):
            self.k_up[dyl, step] = self.wire.send(below, below, me.device(dz=1))
        if step < NZ // 2 - 1 or (step == NZ // 2 - 1 and dyl == 1):
            self.k_down[dyl, step] = self.wire.send(above, above, me.device(dz=-1))
        self.to_sibling(dyl, -step)
        if step:
            self.to_sibling(dyl, step)

    def to_sibling(self, dyl, dz):
        ref = self.plane_ref(dyl, dz)
        self.sib.append((self.wire.send(ref, ref, self.me.device(dc=1)), dyl, dz))

    def step(self, step):
        for dyl in range(NYL):
            if step < NZ // 2:
                self.wire.arrived(self.k_up[dyl, step - 1], self.plane_ref(dyl, -step))
                self.wire.arrived(self.k_down[dyl, step - 1], self.plane_ref(dyl, step))
                self.pass_on(dyl, step)
            else:
                keys = self.k_up if dyl == 0 else self.k_down
                self.wire.arrived(keys[dyl, step - 1], self.plane_ref(dyl, step))
                self.to_sibling(dyl, step)

    def end(self):
        for k, dyl, dz in self.sib:
            self.wire.arrived(k, self.plane_ref(dyl, dz, 1))

    def partners(self):
        me = self.me
        return [
            me.device(dy=2),
            me.device(dx=2),
            me.device(dz=1),
            me.device(dz=-1),
        ] + [me.device(dyl=1, dy=dy) for dy in range(NYH)]


class MetaGather:
    def __init__(self, me, wire, buf):
        self.me, self.wire, self.buf = me, wire, buf

    def column(self, dx):
        x = lax.rem(self.me.x + (dx + NX), NX)
        return self.buf.at[self.me.c, pl.ds(x * NYH, NYH)]

    def begin(self):
        me, self.k = self.me, []
        for dy in (1, -1, 2):
            ref = self.buf.at[me.c, me.chip()]
            self.k.append((self.wire.send(ref, ref, me.device(dy=dy)), dy))

    def columns(self):
        me = self.me
        for k, dy in self.k:
            self.wire.arrived(k, self.buf.at[me.c, me.chip(0, -dy)])
        self.k = []
        for dx in (1, -1, 2):
            ref = self.column(0)
            self.k.append((self.wire.send(ref, ref, me.device(dx=dx)), dx))

    def pair(self):
        for k, dx in self.k:
            self.wire.arrived(k, self.column(-dx))
        ref = self.buf.at[self.me.c]
        self.k_pair = self.wire.send(ref, ref, self.me.device(dc=1))

    def end(self):
        self.wire.arrived(self.k_pair, self.buf.at[1 - self.me.c])


def add_into(dst, *others):
    total = dst[...].astype(jnp.float32)
    for other in others:
        total = total + other[...].astype(jnp.float32)
    dst[...] = total.astype(dst.dtype)


class TermScatter:
    def __init__(self, me, wire, terms, bufs):
        self.me, self.wire, self.terms = me, wire, terms
        (self.pair, self.part, self.far_up, self.far_down, self.near_up, self.near_down,
         self.row, self.yfar_up, self.yfar_down, self.ynear_up, self.ynear_down) = bufs
        self.k_pair = []

    def send_pair(self, group):
        chips = pl.ds(group * NYH, NYH)
        k = self.wire.send(
            self.terms.at[chips, 1 - self.me.c], self.pair.at[chips], self.me.device(dc=1)
        )
        self.k_pair.append((k, group))

    def at_x(self, dx):
        return lax.rem(self.me.x + (dx + NX), NX) * NYH

    def group(self, dx, first, count):
        return self.part.at[pl.ds(self.at_x(dx) + first, count)]

    def along_x(self):
        me, wire = self.me, self.wire
        for k, group in self.k_pair:
            wire.arrived(k, self.pair.at[pl.ds(group * NYH, NYH)])

        @pl.loop(0, NX * NYH)
        def _(i):
            self.part[i] = (
                self.terms[i, me.c].astype(jnp.float32) + self.pair[i].astype(jnp.float32)
            ).astype(jnp.bfloat16)

        half = NYH // 2
        near_up, near_down = self.near_up, self.near_down
        self.a = wire.send(self.group(2, 0, half), self.far_up, me.device(dx=1))
        self.b = wire.send(self.group(2, half, half), self.far_down, me.device(dx=-1))
        self.c = wire.send(
            self.group(1, half, half), near_up.at[pl.ds(half, half)], me.device(dx=1)
        )
        self.d = wire.send(
            self.group(-1, 0, half), near_down.at[pl.ds(0, half)], me.device(dx=-1)
        )

    def x_far(self):
        me, wire = self.me, self.wire
        half = NYH // 2
        wire.arrived(self.a, self.far_up)
        add_into(self.group(1, 0, half), self.far_up)
        self.e = wire.send(
            self.group(1, 0, half), self.near_up.at[pl.ds(0, half)], me.device(dx=1)
        )
        wire.arrived(self.b, self.far_down)
        add_into(self.group(-1, half, half), self.far_down)
        self.f = wire.send(
            self.group(-1, half, half), self.near_down.at[pl.ds(half, half)], me.device(dx=-1)
        )

    def at_y(self, dy):
        return lax.rem(self.me.yh + (dy + NYH), NYH)

    def along_y(self):
        me, wire = self.me, self.wire
        half = NYH // 2
        wire.arrived(self.c, self.near_up.at[pl.ds(half, half)])
        wire.arrived(self.d, self.near_down.at[pl.ds(0, half)])
        wire.arrived(self.e, self.near_up.at[pl.ds(0, half)])
        wire.arrived(self.f, self.near_down.at[pl.ds(half, half)])
        mine = self.at_x(0)
        row = self.row

        @pl.loop(0, NYH)
        def _(i):
            row[i] = (
                self.part[mine + i].astype(jnp.float32)
                + self.near_up[i].astype(jnp.float32)
                + self.near_down[i].astype(jnp.float32)
            ).astype(jnp.bfloat16)

        rows = TOK // 2
        low, high = pl.ds(0, rows), pl.ds(rows, rows)
        at_y = self.at_y
        self.a = wire.send(row.at[at_y(2), low], self.yfar_up, me.device(dy=1))
        self.b = wire.send(row.at[at_y(2), high], self.yfar_down, me.device(dy=-1))
        self.c = wire.send(row.at[at_y(1), high], self.ynear_up.at[high], me.device(dy=1))
        self.d = wire.send(row.at[at_y(-1), low], self.ynear_down.at[low], me.device(dy=-1))

    def y_far(self):
        me, wire, row, at_y = self.me, self.wire, self.row, self.at_y
        rows = TOK // 2
        low, high = pl.ds(0, rows), pl.ds(rows, rows)
        wire.arrived(self.a, self.yfar_up)
        add_into(row.at[at_y(1), low], self.yfar_up)
        self.e = wire.send(row.at[at_y(1), low], self.ynear_up.at[low], me.device(dy=1))
        wire.arrived(self.b, self.yfar_down)
        add_into(row.at[at_y(-1), high], self.yfar_down)
        self.f = wire.send(row.at[at_y(-1), high], self.ynear_down.at[high], me.device(dy=-1))

    def result(self):
        wire = self.wire
        rows = TOK // 2
        low, high = pl.ds(0, rows), pl.ds(rows, rows)
        wire.arrived(self.c, self.ynear_up.at[high])
        wire.arrived(self.d, self.ynear_down.at[low])
        wire.arrived(self.e, self.ynear_up.at[low])
        wire.arrived(self.f, self.ynear_down.at[high])
        return (
            self.row[self.at_y(0)].astype(jnp.float32)
            + self.ynear_up[...].astype(jnp.float32)
            + self.ynear_down[...].astype(jnp.float32)
        )


def dot(a, b, dims):
    return lax.dot_general(a, b, (dims, ((), ())), preferred_element_type=jnp.float32)


NN = ((1,), (0,))
NT = ((1,), (1,))
TN = ((0,), (0,))
F32, B16 = jnp.float32, jnp.bfloat16
SCALE = HD ** (-0.5)
ENC = (R / D) ** 0.5


def row_sum(values):
    return jnp.sum(values, axis=-1, keepdims=True)


def rms_of(total):
    return lax.rsqrt(total * (1.0 / D) + EPS)


def stack_heads(matrix):
    return jnp.concatenate([matrix[:, h * HD : (h + 1) * HD] for h in range(HQ)], axis=0)


def from_columns(columns):
    return jnp.concatenate(
        [columns[:, h * TOK : (h + 1) * TOK].T for h in range(HQ)], axis=1
    )


def to_columns(matrix):
    return jnp.concatenate([matrix[:, h * HD : (h + 1) * HD].T for h in range(HQ)], axis=1)


def tick_kernel(
    codes_ref, saved_ref, grads_ref, docs_f_ref, docs_b_ref, codec_ref, wqkv_ref, wout_ref,
    g1_ref, g2_ref,
    codes_out, grads_out,
    wq, wo, cd, meta, rows, sv, st, gm, mx, kvf, kvb, probs, terms, sent, gin,
    both, other, tile,
    pair, part, far_up, far_down, near_up, near_down, row, yfar_up, yfar_down, ynear_up, ynear_down,
    send_sems, recv_sems, local_sems,
):
    me = Place()
    wire = Wire(send_sems, recv_sems)
    weights = SectionGather(me, wire, wq, TOK)
    outs = SectionGather(me, wire, wo, TOK)
    codec = CodecGather(me, wire, cd, both, other, tile)
    metas = MetaGather(me, wire, meta)
    back = SectionGather(me, wire, kvb, TOK)
    fore = SectionGather(me, wire, kvf, TOK)
    scatter = TermScatter(
        me, wire, terms,
        (pair, part, far_up, far_down, near_up, near_down, row,
         yfar_up, yfar_down, ynear_up, ynear_down),
    )
    own = me.slot()
    sections = NYL * NZ
    after = {"section": lax.rem(me.section + 1, sections), "seq": me.seq}
    before = {"section": lax.rem(me.section + sections - 1, sections), "seq": me.seq}

    fill_q = pltpu.make_async_copy(wqkv_ref.at[0], wq.at[own], local_sems.at[0])
    fill_o = pltpu.make_async_copy(wout_ref.at[0], wo.at[own], local_sems.at[1])
    fill_s = [
        pltpu.make_async_copy(
            saved_ref.at[:, pl.ds(g * GW, GW)], sv.at[g], local_sems.at[3 + g]
        )
        for g in range(NG)
    ]
    for copy in [fill_q, fill_o] + fill_s:
        copy.start()
    tall = codec_ref[...].astype(F32)
    both[...] = jnp.concatenate([tall, tall], axis=0).astype(B16)
    docs_f, docs_b = docs_f_ref[...].astype(F32), docs_b_ref[...].astype(F32)
    meta[me.c, me.chip()] = jnp.concatenate(
        [docs_f, docs_b, g1_ref[...].astype(F32), g2_ref[...].astype(F32), jnp.zeros((4, TOK), F32)],
        axis=0,
    )
    meet(weights.partners() + codec.partners() + [after, before])
    codec.begin()
    fill_q.wait()
    weights.begin()
    metas.begin()
    fill_o.wait()
    for copy in fill_s:
        copy.wait()

    def square_step(g, total):
        values = sv[g].astype(F32)
        return total + row_sum(values * values)

    zero = jnp.zeros((TOK, 1), F32)
    r1b = rms_of(lax.fori_loop(0, NG, square_step, zero))
    codec.pair(local_sems.at[2])
    metas.columns()
    codec.columns()
    weights.y_near()
    metas.pair()
    codec.planes()
    weights.x_near(0)
    weights.y_far()
    codec.step(1)
    outs.begin()
    weights.x_near(-1)
    codec.step(2)
    weights.x_near(1)
    outs.y_near()
    weights.x_near(2)
    metas.end()
    for q in range(NSEQ):
        rows[q // GS, :, q % GS * TOK : (q % GS + 1) * TOK] = meta[q % NC, q // NC]
    codec.step(3)
    for dy in (0, -1, 1, 2):
        weights.x_far(dy)
    outs.x_near(0)
    outs.y_far()
    weights.end()

    def g1(g):
        return rows[g, 2:3, :]

    def g2(g):
        return rows[g, 3:4, :]

    def wq_of(g):
        return wq[pl.ds(g * GS, GS)].reshape(GW, QKV)

    def wo_of(g):
        return wo[pl.ds(g * GS, GS)].reshape(GW, QW)

    def cd_of(g):
        return cd[pl.ds(pl.multiple_of(g * GW, GW), GW), :]

    def project_b(g, total):
        normed = (sv[g].astype(F32) * r1b * g1(g)).astype(B16)
        return total + dot(normed, wq_of(g), NN)

    qkv_b = lax.fori_loop(0, NG, project_b, jnp.zeros((TOK, QKV), F32)).astype(B16)
    kvb[own] = qkv_b[:, QW:]
    q_b = stack_heads(qkv_b[:, :QW])
    back.begin()
    codec.step(4)
    outs.x_near(-1)
    outs.x_near(1)
    outs.x_near(2)
    back.y_near()
    codec.end()

    def decode(g, total):
        stream = dot(codes_ref[...], cd_of(g), NT)
        st[g] = stream
        return total + row_sum(stream * stream)

    r1f = rms_of(lax.fori_loop(0, NG, decode, zero))

    def project_f(g, total):
        normed = (st[g] * r1f * g1(g)).astype(B16)
        return total + dot(normed, wq_of(g), NN)

    qkv_f = lax.fori_loop(0, NG, project_f, jnp.zeros((TOK, QKV), F32)).astype(B16)
    kvf[own] = qkv_f[:, QW:]
    q_f = stack_heads(qkv_f[:, :QW])
    back.x_near(0)
    back.y_far()
    fore.begin()
    for dy in (0, -1, 1, 2):
        outs.x_far(dy)
    back.x_near(-1)
    back.x_near(1)
    back.x_near(2)
    fore.y_near()

    @pl.loop(0, NG)
    def _(g):
        gm[g] = dot(grads_ref[...], cd_of(g), NT) * ENC * g2(g)

    for dy in (0, -1, 1, 2):
        back.x_far(dy)
    outs.end()
    back.end()
    fore.x_near(0)
    fore.y_far()

    q_pos = (own * TOK + lax.broadcasted_iota(jnp.int32, (1, TOK), 1)).astype(F32)
    q_pos = jnp.concatenate([q_pos] * HQ, axis=1)

    def starts(docs, index):
        zeros = D - jnp.sum(rows[:, index : index + 1, :], axis=(0, 2), keepdims=True)[0]
        return jnp.concatenate([docs * zeros] * HQ, axis=1)

    def keys_of(kv, i):
        return kv[pl.ds(i * KS, KS), :, :HD].reshape(KEYS, HD)

    def values_of(kv, i):
        return kv[pl.ds(i * KS, KS), :, HD:].reshape(KEYS, HD)

    def tops(kv, queries, start):
        def step(i, top):
            scores = dot(keys_of(kv, i), queries, NT) * SCALE
            k_pos = (
                i * KEYS + lax.broadcasted_iota(jnp.int32, (KEYS, HQ * TOK), 0)
            ).astype(F32)
            scores = jnp.where((k_pos >= start) & (k_pos <= q_pos), scores, -1e30)
            probs[i] = scores
            return jnp.maximum(top, jnp.max(scores, axis=0, keepdims=True))

        return lax.fori_loop(0, NK, step, jnp.full((1, HQ * TOK), -1e30, F32))

    def attended(kv, top):
        def step(i, carry):
            total, accum = carry
            p = jnp.exp(probs[i] - top)
            probs[i] = p
            total = total + jnp.sum(p, axis=0, keepdims=True)
            return total, accum + dot(values_of(kv, i), p.astype(B16), TN)

        total, accum = lax.fori_loop(
            0, NK, step, (jnp.zeros((1, HQ * TOK), F32), jnp.zeros((HD, HQ * TOK), F32))
        )
        return total, (accum / total).astype(B16)

    top = tops(kvb, q_b, starts(docs_b, 1))
    fore.x_near(-1)
    fore.x_near(1)
    fore.x_near(2)
    denom, att_cols = attended(kvb, top)
    att_cols = att_cols.astype(F32)
    att = from_columns(att_cols).astype(B16)

    def mix_b(g, carry):
        squares, cross = carry
        mixed = sv[g].astype(F32) + dot(att, wo_of(g), NT)
        mx[g] = mixed
        return squares + row_sum(mixed * mixed), cross + row_sum(mixed * gm[g])

    squares, cross = lax.fori_loop(0, NG, mix_b, (zero, zero))
    for dy in (0, -1, 1, 2):
        fore.x_far(dy)
    r2b = rms_of(squares)
    lean = r2b * r2b * cross * (1.0 / D)

    def grad_mix(g, total):
        grad = r2b * (gm[g] - mx[g] * lean)
        gm[g] = grad
        return total + dot(grad.astype(B16), wo_of(g), NN)

    grad_att = lax.fori_loop(0, NG, grad_mix, jnp.zeros((TOK, QW), F32)).astype(B16)
    g_heads = stack_heads(grad_att)
    delta = jnp.sum(to_columns(grad_att.astype(F32)) * att_cols, axis=0, keepdims=True)
    inverse = 1.0 / denom

    def backward_step(i, total):
        p = probs[i] * inverse
        grad_p = dot(values_of(kvb, i), g_heads, NT)
        grad_s = (p * (grad_p - delta) * SCALE).astype(B16)
        chips = pl.ds(i * (KS // NC), KS // NC)
        shape = (KS // NC, NC, TOK, HD)
        terms[chips, :, :, :HD] = dot(grad_s, q_b, NN).astype(B16).reshape(shape)
        terms[chips, :, :, HD:] = dot(p.astype(B16), g_heads, NN).astype(B16).reshape(shape)
        return total + dot(keys_of(kvb, i), grad_s, TN)

    grad_q = jnp.zeros((HD, HQ * TOK), F32)
    per = NK // NG
    for g in range(NG):
        grad_q = lax.fori_loop(g * per, (g + 1) * per, backward_step, grad_q)
        scatter.send_pair(g)
    grad_q = from_columns(grad_q).astype(B16)
    fore.end()
    scatter.along_x()

    top = tops(kvf, q_f, starts(docs_f, 0))
    scatter.x_far()
    _, att_cols = attended(kvf, top)
    att = from_columns(att_cols.astype(F32)).astype(B16)
    scatter.along_y()

    def mix_f(g, total):
        mixed = st[g] + dot(att, wo_of(g), NT)
        st[g] = mixed
        return total + row_sum(mixed * mixed)

    r2f = rms_of(lax.fori_loop(0, NG, mix_f, zero))
    scatter.y_far()

    def encode(g, total):
        normed = (st[g] * r2f * g2(g)).astype(B16)
        return total + dot(normed, cd_of(g), NN)

    coded = lax.fori_loop(0, NG, encode, jnp.zeros((TOK, R), F32))
    sent[...] = (coded * ENC).astype(B16)
    k_codes = wire.send(sent, codes_out, after)

    kv_grad = scatter.result().astype(B16)
    grad_qkv = jnp.concatenate([grad_q, kv_grad], axis=1)

    def grad_norm(g, total):
        weighted = dot(grad_qkv, wq_of(g), NT) * g1(g)
        mx[g] = weighted
        return total + row_sum(weighted * sv[g].astype(F32))

    cross = lax.fori_loop(0, NG, grad_norm, zero)
    lean1 = r1b * r1b * cross * (1.0 / D)

    def grad_code(g, total):
        grad = gm[g] + r1b * (mx[g] - sv[g].astype(F32) * lean1)
        return total + dot(grad.astype(B16), cd_of(g), NN)

    gin[...] = lax.fori_loop(0, NG, grad_code, jnp.zeros((TOK, R), F32)).astype(B16)
    k_grads = wire.send(gin, grads_out, before)
    wire.arrived(k_codes, codes_out)
    wire.arrived(k_grads, grads_out)
    wire.finish()


ANY = pl.BlockSpec(memory_space=pl.ANY)
VMEM = pl.BlockSpec(memory_space=pltpu.VMEM)


def on_device(
    codes_fwd, saved_stream, grad_codes, docs_fwd, docs_bwd, codec, wqkv, wout, gain_attn, gain_code
):
    copies = 288
    half = NYH // 2
    codes, grads = pl.pallas_call(
        tick_kernel,
        out_shape=(jax.ShapeDtypeStruct((TOK, R), B16),) * 2,
        in_specs=[VMEM, ANY, VMEM, VMEM, VMEM, VMEM, ANY, ANY, VMEM, VMEM],
        out_specs=(VMEM, VMEM),
        scratch_shapes=[
            pltpu.VMEM((NSEQ, TOK, QKV), B16),
            pltpu.VMEM((NSEQ, TOK, QW), B16),
            pltpu.VMEM((D, R), B16),
            pltpu.VMEM((NC, NX * NYH, 8, TOK), F32),
            pltpu.VMEM((NG, 8, GW), F32),
            pltpu.VMEM((NG, TOK, GW), B16),
            pltpu.VMEM((NG, TOK, GW), F32),
            pltpu.VMEM((NG, TOK, GW), F32),
            pltpu.VMEM((NG, TOK, GW), F32),
            pltpu.VMEM((NSEQ, TOK, 2 * HD), B16),
            pltpu.VMEM((NSEQ, TOK, 2 * HD), B16),
            pltpu.VMEM((NK, KEYS, HQ * TOK), F32),
            pltpu.VMEM((NX * NYH, NC, TOK, 2 * HD), B16),
            pltpu.VMEM((TOK, R), B16),
            pltpu.VMEM((TOK, R), B16),
            pltpu.VMEM((CROWS, R), B16),
            pltpu.VMEM((CROWS, R), B16),
            pltpu.VMEM((CROWS, R), B16),
            pltpu.VMEM((NX * NYH, TOK, 2 * HD), B16),
            pltpu.VMEM((NX * NYH, TOK, 2 * HD), B16),
            pltpu.VMEM((half, TOK, 2 * HD), B16),
            pltpu.VMEM((half, TOK, 2 * HD), B16),
            pltpu.VMEM((NYH, TOK, 2 * HD), B16),
            pltpu.VMEM((NYH, TOK, 2 * HD), B16),
            pltpu.VMEM((NYH, TOK, 2 * HD), B16),
            pltpu.VMEM((TOK // 2, 2 * HD), B16),
            pltpu.VMEM((TOK // 2, 2 * HD), B16),
            pltpu.VMEM((TOK, 2 * HD), B16),
            pltpu.VMEM((TOK, 2 * HD), B16),
            pltpu.SemaphoreType.DMA((copies,)),
            pltpu.SemaphoreType.DMA((copies,)),
            pltpu.SemaphoreType.DMA((3 + NG,)),
        ],
        compiler_params=pltpu.CompilerParams(
            collective_id=0, has_side_effects=True, vmem_limit_bytes=56 * 2**20
        ),
        name="tick",
    )(
        codes_fwd[0], saved_stream[0], grad_codes[0], docs_fwd, docs_bwd, codec, wqkv, wout,
        gain_attn, gain_code,
    )
    return codes[None], grads[None]


def solution(mesh):
    return jax.shard_map(
        on_device,
        mesh=mesh,
        in_specs=(
            P("section", "seq", None),
            P("section", "seq", None),
            P("section", "seq", None),
            P("section", "seq"),
            P("section", "seq"),
            P(("section", "seq"), None),
            P("section", "seq", None),
            P("section", "seq", None),
            P("section", "seq"),
            P("section", "seq"),
        ),
        out_specs=(P("section", "seq", None), P("section", "seq", None)),
        check_vma=False,
    )
```

time: 202 us -> 124 us (0.61)
  matrix products: 49.2 us -> 0 us
  starting transfers between devices: 7.7 us -> 0 us
  other arithmetic: 6.35 us -> 0 us
  Pallas kernels: 125 us -> 119 us
  local copies, waits for them, and re-layouts: 7.64 us -> 2.26 us
    dot_general x16 -> x0, matrix products: 40.2 us -> none  [the longest x2 7.9 us: attend(): jnp.einsum('hts,sd->htd', probs.astype(jnp.bfloat16), values, preferred_e...]
    sub x2 -> x0, matrix products: 9.01 us -> none  [attend(): probs = jnp.where(allowed, jnp.exp(masked - top), 0.0)]
    ppermute x2 -> x0, starting transfers between devices: 7.7 us -> none  [shifted(): return lax.ppermute(value, axis, pairs)]
    pallas_call x3 -> x1, Pallas kernels: 125 us -> 119 us  [on_device(): pl.pallas_call(tick_kernel, out_shape=(jax.ShapeDtypeStruct((TOK, R), B16...]
    unnamed x49 -> x4, local copies, waits for them, and re-layouts: 6.31 us -> 2.26 us
    concatenate x2 -> x0, other arithmetic: 2.48 us -> none  [the longest x1 1.81 us: on_device(): jnp.concatenate([key_term, value_term], axis=1).astype(jnp.bfloat16)]
  transfers between devices with their start and end apart: 2 -> 0, of which waited for: 1 -> 0; matrix products, arithmetic and copies ran while one was open for 17% -> 0% of each run, Pallas kernels for 12% -> 0%
where the time goes in v2:
time: 124 us; the launch traced here: 122 us
  Pallas kernels  119 us (96%)
  local copies, waits for them, and re-layouts  2.26 us (2%)
    pallas_call x1, Pallas kernels, on_device(): pl.pallas_call(tick_kernel, out_shape=(jax.ShapeDtypeStruct((TOK, R), B16...  119 us

profile of v2, /device:TPU:1, one launch (start us, length us, event | category | flops | bytes accessed | tf_op | source)
XLA Modules:
  0.0 121.8 jit_solution(12310791324395173420)
XLA Ops:
  0.6 118.9 %tick.1 = (bf16[128,512]{1,0:T(8,128)(2,1)}, bf16[128,512]{1,0:T(8,128)(2,1)}) custom-call(bf16[128,512]{1,0:T(8,128)(2,1)} %bitcast.6, bf16[128,4096]{1,0:T(8,128)(2,1)} %bitcast.5, bf16[128,512]{1,0:T(8,128)(2,1)} %bitcast.7, s32[1,128]{1,0:T(1,128)} %docs_f_ref.1, s32[1,128]{1,0:T(1,128)} %docs_b_ref.1, bf16[8,512]{1,0:T(8,128)(2,1)} %codec_ref.1, ...), custom_call_target="tpu_custom_call" | custom-call | tf_op jit(solution)/shard_map/tick/pallas_call | solution.py:752
  119.5 0.0 copy-start
  119.5 1.6 %copy.14 = bf16[1,128,512]{2,1,0:T(8,128)(2,1)} copy(bf16[1,128,512]{2,1,0:T(8,128)(2,1)} %bitcast.9) | data formatting | bytes 262144
  121.1 0.0 copy-done
  121.1 0.7 copy.15
Async XLA Ops:
  119.5 1.6 %copy-start = (bf16[128,512]{1,0:T(8,128)(2,1)S(1)}, bf16[128,512]{1,0:T(8,128)(2,1)}, u32[]{:S(2)}) copy-start(bf16[128,512]{1,0:T(8,128)(2,1)} %get-tuple-element.5) | copy-start | bytes 393220

commit v3 on v2

v3 whole, which is shorter than its diff:
```python
import functools

import jax
import jax.numpy as jnp
from jax import lax
from jax.experimental import pallas as pl
from jax.experimental.pallas import tpu as pltpu
from jax.sharding import PartitionSpec as P

D = 4096
R = 512
HD = 128
HQ = 2
TOK = 128
QKV = (HQ + 2) * HD
QW = HQ * HD
NX, NYH, NC = 4, 4, 2
NYL, NZ = 2, 8
NSEQ = NX * NYH * NC
NG = NX
GW = D // NG
GS = NSEQ // NG
KEYS = 512
KS = KEYS // TOK
NK = D // KEYS
SEMAPHORES = 4 * 17 + 21 + 5 + 19 + 4

EPS = 1e-05


class Place:
    def __init__(self):
        self.section = lax.axis_index("section")
        self.seq = lax.axis_index("seq")
        self.ylo = self.section // NZ
        self.z = lax.rem(self.section, NZ)
        self.x = self.seq // (NYH * NC)
        self.yh = lax.rem(self.seq // NC, NYH)
        self.c = lax.rem(self.seq, NC)

    def slot(self, dx=0, dy=0, dc=0):
        x = lax.rem(self.x + (dx + NX), NX)
        yh = lax.rem(self.yh + (dy + NYH), NYH)
        c = lax.rem(self.c + dc, NC)
        return (x * NYH + yh) * NC + c

    def chip(self, dx=0, dy=0):
        return lax.rem(self.x + (dx + NX), NX) * NYH + lax.rem(self.yh + (dy + NYH), NYH)

    def device(self, dx=0, dy=0, dc=0, dz=0, dyl=0):
        z = lax.rem(self.z + (dz + NZ), NZ)
        ylo = lax.rem(self.ylo + dyl, NYL)
        return {"section": ylo * NZ + z, "seq": self.slot(dx, dy, dc)}


class Wire:
    def __init__(self, sems):
        self.sems, self.used = sems, 0

    def new(self):
        self.used += 1
        assert self.used <= SEMAPHORES
        return self.used - 1

    def send(self, src, dst, device, out, into):
        pltpu.make_async_remote_copy(
            src_ref=src,
            dst_ref=dst,
            send_sem=self.sems.at[out],
            recv_sem=self.sems.at[into],
            device_id=device,
            device_id_type=pl.DeviceIdType.MESH,
        ).start()

    def take(self, k, ref):
        pltpu.make_async_copy(ref, ref, self.sems.at[k]).wait()


def meet(devices):
    barrier = pltpu.get_barrier_semaphore()
    for device in devices:
        pl.semaphore_signal(barrier, inc=1, device_id=device, device_id_type=pl.DeviceIdType.MESH)
    pl.semaphore_wait(barrier, len(devices))


class SectionGather:
    def __init__(self, me, wire, out, rows):
        self.me, self.wire, self.out = me, wire, out
        self.half = rows // 2
        self.sent = wire.new()
        self.y_up, self.y_down, self.y_two, self.sib = [wire.new() for _ in range(4)]
        self.x_up = {dy: wire.new() for dy in (0, -1, 1, 2)}
        self.x_down = {dy: wire.new() for dy in (0, -1, 1, 2)}
        self.x_two = {dy: wire.new() for dy in (0, -1, 1, 2)}

    def block(self, dx, dy):
        return self.out.at[self.me.slot(dx, dy)]

    def part(self, dx, dy, which):
        return self.out.at[self.me.slot(dx, dy), pl.ds(which * self.half, self.half)]

    def push(self, ref, into, **to):
        self.wire.send(ref, ref, self.me.device(**to), self.sent, into)

    def to_sibling(self, dx, dy):
        self.push(self.block(dx, dy), self.sib, dc=1)

    def begin(self):
        self.begin_y()
        self.begin_x()

    def begin_y(self):
        self.push(self.block(0, 0), self.y_up, dy=1)
        self.push(self.block(0, 0), self.y_down, dy=-1)

    def begin_x(self):
        self.along_x(0)
        self.to_sibling(0, 0)

    def along_x(self, dy):
        self.push(self.block(0, dy), self.x_up[dy], dx=1)
        self.push(self.block(0, dy), self.x_down[dy], dx=-1)

    def y_near(self):
        self.wire.take(self.y_up, self.block(0, -1))
        self.push(self.part(0, -1, 0), self.y_two, dy=1)
        self.along_x(-1)
        self.wire.take(self.y_down, self.block(0, 1))
        self.push(self.part(0, 1, 1), self.y_two, dy=-1)
        self.along_x(1)
        self.to_sibling(0, -1)
        self.to_sibling(0, 1)

    def y_far(self):
        self.wire.take(self.y_two, self.block(0, 2))
        self.along_x(2)
        self.to_sibling(0, 2)

    def x_near(self, dy):
        self.wire.take(self.x_up[dy], self.block(-1, dy))
        self.push(self.part(-1, dy, 0), self.x_two[dy], dx=1)
        self.wire.take(self.x_down[dy], self.block(1, dy))
        self.push(self.part(1, dy, 1), self.x_two[dy], dx=-1)
        self.to_sibling(-1, dy)
        self.to_sibling(1, dy)

    def x_far(self, *rows):
        for dy in rows:
            self.wire.take(self.x_two[dy], self.block(2, dy))
            self.to_sibling(2, dy)

    def end(self):
        self.wire.take(self.sib, self.out.at[pl.ds(0, NX * NYH)])

    def finish(self):
        self.wire.take(self.sent, self.out.at[pl.ds(0, NSEQ - 1)])

    def partners(self):
        me = self.me
        return [
            me.device(dy=1),
            me.device(dy=-1),
            me.device(dx=1),
            me.device(dx=-1),
            me.device(dc=1),
        ]


CROWS = 16
PLANE = NX * NYH * CROWS
LANES = R // NC


class CodecGather:
    def __init__(self, me, wire, out, both, other, tile):
        self.me, self.wire, self.out = me, wire, out
        self.both, self.other, self.tile = both, other, tile
        new = wire.new
        self.pair_out, self.pair_in, self.sent, self.sib_out, self.sib = [new() for _ in range(5)]
        self.in_y, self.in_x = new(), new()
        self.up, self.down = {}, {}
        for step in range(1, NZ // 2 + 1):
            for dyl in range(NYL):
                if step < NZ // 2 or dyl == 0:
                    self.up[dyl, step] = new()
                if step < NZ // 2 or dyl == 1:
                    self.down[dyl, step] = new()

    def ref(self, first, rows, dc=0):
        c = lax.rem(self.me.c + dc, NC)
        return self.out.at[
            pl.ds(pl.multiple_of(first, CROWS), rows),
            pl.ds(pl.multiple_of(c * LANES, LANES), LANES),
        ]

    def plane_first(self, dyl, dz):
        me = self.me
        ylo = lax.rem(me.ylo + dyl, NYL)
        return (ylo * NZ + lax.rem(me.z + (dz + NZ), NZ)) * PLANE

    def tile_ref(self, dyl, dy):
        return self.ref(self.plane_first(dyl, 0) + self.me.chip(0, dy) * CROWS, CROWS)

    def column_ref(self, dyl, dx):
        x = lax.rem(self.me.x + (dx + NX), NX)
        return self.ref(self.plane_first(dyl, 0) + x * (NYH * CROWS), NYH * CROWS)

    def plane_ref(self, dyl, dz, dc=0):
        return self.ref(self.plane_first(dyl, dz), PLANE, dc)

    def begin(self):
        me = self.me
        self.wire.send(self.both, self.other, me.device(dc=1), self.pair_out, self.pair_in)

    def pair(self, local_sem):
        me = self.me
        self.wire.take(self.pair_in, self.other)
        row = lax.broadcasted_iota(jnp.int32, (CROWS, R), 0)
        mine = (row // (CROWS // NC)) == me.c
        self.tile[...] = jnp.where(
            mine, self.both[...].astype(jnp.float32), self.other[...].astype(jnp.float32)
        ).astype(jnp.bfloat16)
        src = self.tile.at[:, pl.ds(pl.multiple_of(me.c * LANES, LANES), LANES)]
        self.local = pltpu.make_async_copy(src, self.tile_ref(0, 0), local_sem)
        self.local.start()
        for dyl in range(NYL):
            for dy in range(NYH):
                if dyl or dy:
                    to = me.device(dy=dy, dyl=dyl)
                    self.wire.send(src, self.tile_ref(0, 0), to, self.sent, self.in_y)

    def columns(self):
        me = self.me
        self.local.wait()
        self.wire.take(self.in_y, self.out.at[pl.ds(0, (NYL * NYH - 1) * CROWS), pl.ds(0, LANES)])
        for dx in (1, -1, 2):
            for dyl in range(NYL):
                ref = self.column_ref(dyl, 0)
                self.wire.send(ref, ref, me.device(dx=dx), self.sent, self.in_x)

    def planes(self):
        rows = (NX - 1) * NYL * NYH * CROWS
        self.wire.take(self.in_x, self.out.at[pl.ds(0, rows), pl.ds(0, LANES)])
        for dyl in range(NYL):
            self.pass_on(dyl, 0)

    def pass_on(self, dyl, step):
        me = self.me
        below, above = self.plane_ref(dyl, -step), self.plane_ref(dyl, step)
        if (dyl, step + 1) in self.up:
            self.wire.send(below, below, me.device(dz=1), self.sent, self.up[dyl, step + 1])
        if (dyl, step + 1) in self.down:
            self.wire.send(above, above, me.device(dz=-1), self.sent, self.down[dyl, step + 1])
        self.to_sibling(dyl, -step)
        if step:
            self.to_sibling(dyl, step)

    def to_sibling(self, dyl, dz):
        ref = self.plane_ref(dyl, dz)
        self.wire.send(ref, ref, self.me.device(dc=1), self.sib_out, self.sib)

    def step(self, step):
        for dyl in range(NYL):
            if step < NZ // 2:
                self.wire.take(self.up[dyl, step], self.plane_ref(dyl, -step))
                self.wire.take(self.down[dyl, step], self.plane_ref(dyl, step))
                self.pass_on(dyl, step)
            else:
                keys = self.up if dyl == 0 else self.down
                self.wire.take(keys[dyl, step], self.plane_ref(dyl, step))
                self.to_sibling(dyl, step)

    def end(self):
        self.wire.take(self.sib, self.out.at[:, pl.ds(0, LANES)])

    def finish(self):
        rows = 7 * CROWS + 6 * NYH * CROWS + 14 * PLANE
        self.wire.take(self.pair_out, self.both)
        self.wire.take(self.sent, self.out.at[pl.ds(0, rows), pl.ds(0, LANES)])
        self.wire.take(self.sib_out, self.out.at[:, pl.ds(0, LANES)])

    def partners(self):
        me = self.me
        return [
            me.device(dy=2),
            me.device(dx=2),
            me.device(dz=1),
            me.device(dz=-1),
        ] + [me.device(dyl=1, dy=dy) for dy in range(NYH)]


class MetaGather:
    def __init__(self, me, wire, buf):
        self.me, self.wire, self.buf = me, wire, buf
        self.sent, self.in_y, self.in_x, self.sib_out, self.sib = [wire.new() for _ in range(5)]

    def column(self, dx):
        x = lax.rem(self.me.x + (dx + NX), NX)
        return self.buf.at[self.me.c, pl.ds(x * NYH, NYH)]

    def begin(self):
        me = self.me
        ref = self.buf.at[me.c, me.chip()]
        for dy in (1, -1, 2):
            self.wire.send(ref, ref, me.device(dy=dy), self.sent, self.in_y)

    def columns(self):
        me = self.me
        self.wire.take(self.in_y, self.buf.at[0, pl.ds(0, NYH - 1)])
        ref = self.column(0)
        for dx in (1, -1, 2):
            self.wire.send(ref, ref, me.device(dx=dx), self.sent, self.in_x)

    def pair(self):
        me = self.me
        self.wire.take(self.in_x, self.buf.at[0, pl.ds(0, (NX - 1) * NYH)])
        ref = self.buf.at[me.c]
        self.wire.send(ref, ref, me.device(dc=1), self.sib_out, self.sib)

    def end(self):
        self.wire.take(self.sib, self.buf.at[0])

    def finish(self):
        self.wire.take(self.sent, self.buf.at[0, pl.ds(0, NYH - 1 + (NX - 1) * NYH)])
        self.wire.take(self.sib_out, self.buf.at[0])


def add_into(dst, *others):
    total = dst[...].astype(jnp.float32)
    for other in others:
        total = total + other[...].astype(jnp.float32)
    dst[...] = total.astype(dst.dtype)


class TermScatter:
    def __init__(self, me, wire, terms, bufs):
        self.me, self.wire, self.terms = me, wire, terms
        (self.pair, self.part, self.far_up, self.far_down, self.near_up, self.near_down,
         self.row, self.yfar_up, self.yfar_down, self.ynear_up, self.ynear_down) = bufs
        new = wire.new
        self.pair_out, self.x_out, self.y_out = new(), new(), new()
        self.pair_in = {dx: new() for dx in (2, 1, -1, 0)}
        self.x_in, self.y_in = [new() for _ in range(6)], [new() for _ in range(6)]

    def at_x(self, dx):
        return lax.rem(self.me.x + (dx + NX), NX) * NYH

    def group(self, dx, first=0, count=NYH):
        return self.part.at[pl.ds(self.at_x(dx) + first, count)]

    def send_pair(self, dx):
        chips = pl.ds(self.at_x(dx), NYH)
        self.wire.send(
            self.terms.at[chips, 1 - self.me.c], self.pair.at[chips],
            self.me.device(dc=1), self.pair_out, self.pair_in[dx],
        )

    def add_pair(self, dx):
        first = self.at_x(dx)
        self.wire.take(self.pair_in[dx], self.pair.at[pl.ds(first, NYH)])
        for j in range(NYH):
            i = first + j
            self.part[i] = (
                self.terms[i, self.me.c].astype(jnp.float32) + self.pair[i].astype(jnp.float32)
            ).astype(jnp.bfloat16)

    def send_x(self, src, dst, k, dx):
        self.wire.send(src, dst, self.me.device(dx=dx), self.x_out, self.x_in[k])

    def x_start(self):
        half = NYH // 2
        self.send_x(self.group(2, 0, half), self.far_up, 0, 1)
        self.send_x(self.group(2, half, half), self.far_down, 1, -1)

    def x_up(self):
        half = NYH // 2
        self.send_x(self.group(1, half, half), self.near_up.at[pl.ds(half, half)], 2, 1)

    def x_down(self):
        half = NYH // 2
        self.send_x(self.group(-1, 0, half), self.near_down.at[pl.ds(0, half)], 3, -1)

    def x_far(self):
        half = NYH // 2
        self.wire.take(self.x_in[0], self.far_up)
        add_into(self.group(1, 0, half), self.far_up)
        self.send_x(self.group(1, 0, half), self.near_up.at[pl.ds(0, half)], 4, 1)
        self.wire.take(self.x_in[1], self.far_down)
        add_into(self.group(-1, half, half), self.far_down)
        self.send_x(self.group(-1, half, half), self.near_down.at[pl.ds(half, half)], 5, -1)

    def at_y(self, dy):
        return lax.rem(self.me.yh + (dy + NYH), NYH)

    def send_y(self, src, dst, k, dy):
        self.wire.send(src, dst, self.me.device(dy=dy), self.y_out, self.y_in[k])

    def along_y(self):
        half = NYH // 2
        for k, ref in ((2, self.near_up), (3, self.near_down), (4, self.near_up), (5, self.near_down)):
            self.wire.take(self.x_in[k], ref.at[pl.ds(0, half)])
        mine = self.at_x(0)
        row = self.row
        for i in range(NYH):
            row[i] = (
                self.part[mine + i].astype(jnp.float32)
                + self.near_up[i].astype(jnp.float32)
                + self.near_down[i].astype(jnp.float32)
            ).astype(jnp.bfloat16)
        rows = TOK // 2
        low, high = pl.ds(0, rows), pl.ds(rows, rows)
        at_y = self.at_y
        self.send_y(row.at[at_y(2), low], self.yfar_up, 0, 1)
        self.send_y(row.at[at_y(2), high], self.yfar_down, 1, -1)
        self.send_y(row.at[at_y(1), high], self.ynear_up.at[high], 2, 1)
        self.send_y(row.at[at_y(-1), low], self.ynear_down.at[low], 3, -1)

    def y_far(self):
        row, at_y = self.row, self.at_y
        rows = TOK // 2
        low, high = pl.ds(0, rows), pl.ds(rows, rows)
        self.wire.take(self.y_in[0], self.yfar_up)
        add_into(row.at[at_y(1), low], self.yfar_up)
        self.send_y(row.at[at_y(1), low], self.ynear_up.at[low], 4, 1)
        self.wire.take(self.y_in[1], self.yfar_down)
        add_into(row.at[at_y(-1), high], self.yfar_down)
        self.send_y(row.at[at_y(-1), high], self.ynear_down.at[high], 5, -1)

    def result(self):
        rows = TOK // 2
        low, high = pl.ds(0, rows), pl.ds(rows, rows)
        self.wire.take(self.y_in[2], self.ynear_up.at[high])
        self.wire.take(self.y_in[3], self.ynear_down.at[low])
        self.wire.take(self.y_in[4], self.ynear_up.at[low])
        self.wire.take(self.y_in[5], self.ynear_down.at[high])
        return (
            self.row[self.at_y(0)].astype(jnp.float32)
            + self.ynear_up[...].astype(jnp.float32)
            + self.ynear_down[...].astype(jnp.float32)
        )

    def finish(self):
        self.wire.take(self.pair_out, self.pair)
        self.wire.take(self.x_out, self.part.at[pl.ds(0, NX * NYH - NYH)])
        self.wire.take(self.y_out, self.row.at[pl.ds(0, NYH - 1)])


def dot(a, b, dims):
    return lax.dot_general(a, b, (dims, ((), ())), preferred_element_type=jnp.float32)


NN = ((1,), (0,))
NT = ((1,), (1,))
TN = ((0,), (0,))
F32, B16 = jnp.float32, jnp.bfloat16
SCALE = HD ** (-0.5)
ENC = (R / D) ** 0.5


def row_sum(values):
    return jnp.sum(values, axis=-1, keepdims=True)


def rms_of(total):
    return lax.rsqrt(total * (1.0 / D) + EPS)


def stack_heads(matrix):
    return jnp.concatenate([matrix[:, h * HD : (h + 1) * HD] for h in range(HQ)], axis=0)


def from_columns(columns):
    return jnp.concatenate(
        [columns[:, h * TOK : (h + 1) * TOK].T for h in range(HQ)], axis=1
    )


def to_columns(matrix):
    return jnp.concatenate([matrix[:, h * HD : (h + 1) * HD].T for h in range(HQ)], axis=1)


def tick_kernel(
    codes_ref, saved_ref, grads_ref, docs_f_ref, docs_b_ref, codec_ref, wqkv_ref, wout_ref,
    g1_ref, g2_ref,
    codes_out, grads_out,
    wk, wo, cd, meta, rows, sv, nb, st, gm, mx, kvf, kvb, probs, terms, codes, grads, sent, gin,
    both, other, tile,
    pair, part, far_up, far_down, near_up, near_down, row, yfar_up, yfar_down, ynear_up, ynear_down,
    sems, local_sems,
):
    me = Place()
    wire = Wire(sems)
    first = SectionGather(me, wire, wk, TOK)
    second = SectionGather(me, wire, wo, TOK)
    codec = CodecGather(me, wire, cd, both, other, tile)
    metas = MetaGather(me, wire, meta)
    back = SectionGather(me, wire, kvb, TOK)
    fore = SectionGather(me, wire, kvf, TOK)
    scatter = TermScatter(
        me, wire, terms,
        (pair, part, far_up, far_down, near_up, near_down, row,
         yfar_up, yfar_down, ynear_up, ynear_down),
    )
    codes_sent, codes_in, grads_sent, grads_in = [wire.new() for _ in range(4)]
    own = me.slot()
    sections = NYL * NZ
    after = {"section": lax.rem(me.section + 1, sections), "seq": me.seq}
    before = {"section": lax.rem(me.section + sections - 1, sections), "seq": me.seq}
    everyone = (0, -1, 1, 2)

    fills = []

    def fill(src, dst):
        copy = pltpu.make_async_copy(src, dst, local_sems.at[len(fills)])
        copy.start()
        fills.append(copy)
        return copy

    fill_k = fill(wqkv_ref.at[0, :, pl.ds(QW, 2 * HD)], wk.at[own])
    fill_w = [
        fill(wqkv_ref.at[0, :, pl.ds(0, QW)], wo.at[own, :, pl.ds(0, QW)]),
        fill(wout_ref.at[0], wo.at[own, :, pl.ds(QW, QW)]),
    ]
    fill_x = [fill(saved_ref.at[:, pl.ds(g * GW, GW)], sv.at[g]) for g in range(NG)]
    fill_x += [fill(codes_ref, codes), fill(grads_ref, grads)]
    tall = codec_ref[...].astype(F32)
    both[...] = jnp.concatenate([tall, tall], axis=0).astype(B16)
    docs_f, docs_b = docs_f_ref[...].astype(F32), docs_b_ref[...].astype(F32)
    meta[me.c, me.chip()] = jnp.concatenate(
        [docs_f, docs_b, g1_ref[...].astype(F32), g2_ref[...].astype(F32), jnp.zeros((4, TOK), F32)],
        axis=0,
    )
    meet(first.partners() + codec.partners() + [after, before])
    fill_k.wait()
    first.begin()
    codec.begin()
    metas.begin()
    for copy in fill_w:
        copy.wait()
    second.begin_x()
    for copy in fill_x:
        copy.wait()

    def square_step(g, total):
        values = sv[g].astype(F32)
        return total + row_sum(values * values)

    zero = jnp.zeros((TOK, 1), F32)
    codec.pair(local_sems.at[len(fills)])
    r1b = rms_of(lax.fori_loop(0, NG, square_step, zero))
    metas.columns()
    first.x_near(0)
    first.y_near()
    second.begin_y()
    codec.columns()
    second.x_near(0)
    metas.pair()
    first.y_far()
    first.x_near(-1)
    first.x_near(1)
    codec.planes()
    metas.end()
    for q in range(NSEQ):
        rows[q // GS, :, q % GS * TOK : (q % GS + 1) * TOK] = meta[q % NC, q // NC]

    def g1(g):
        return rows[g, 2:3, :]

    def g2(g):
        return rows[g, 3:4, :]

    @pl.loop(0, NG)
    def _(g):
        nb[g] = (sv[g].astype(F32) * r1b * g1(g)).astype(B16)

    first.x_far(0)
    first.x_near(2)
    second.y_near()
    first.x_far(-1, 1, 2)
    first.end()

    def wk_of(g):
        return wk[pl.ds(g * GS, GS)].reshape(GW, 2 * HD)

    def wq_of(g):
        return wo[pl.ds(g * GS, GS), :, :QW].reshape(GW, QW)

    def wo_of(g):
        return wo[pl.ds(g * GS, GS), :, QW:].reshape(GW, QW)

    def cd_of(g):
        return cd[pl.ds(pl.multiple_of(g * GW, GW), GW), :]

    def project(values, weights_of):
        def step(g, total):
            return total + dot(values[g], weights_of(g), NN)

        return lax.fori_loop(0, NG, step, jnp.zeros((TOK, QW), F32)).astype(B16)

    kvb[own] = project(nb, wk_of)
    back.begin()
    second.y_far()
    second.x_near(-1)
    second.x_near(1)
    codec.step(1)
    back.x_near(0)
    back.y_near()
    second.x_near(2)
    codec.step(2)
    back.y_far()
    second.x_far(*everyone)
    back.x_near(-1)
    back.x_near(1)
    codec.step(3)
    back.x_near(2)
    second.end()
    q_b = stack_heads(project(nb, wq_of))
    back.x_far(*everyone)
    codec.step(4)
    codec.end()

    def decode(g, total):
        stream = dot(codes[...], cd_of(g), NT)
        st[g] = stream
        return total + row_sum(stream * stream)

    r1f = rms_of(lax.fori_loop(0, NG, decode, zero))

    @pl.loop(0, NG)
    def _(g):
        nb[g] = (st[g] * r1f * g1(g)).astype(B16)

    kvf[own] = project(nb, wk_of)
    fore.begin()
    q_f = stack_heads(project(nb, wq_of))
    back.end()

    q_pos = (own * TOK + lax.broadcasted_iota(jnp.int32, (1, TOK), 1)).astype(F32)
    q_pos = jnp.concatenate([q_pos] * HQ, axis=1)

    def starts(docs, index):
        zeros = D - jnp.sum(rows[:, index : index + 1, :], axis=(0, 2), keepdims=True)[0]
        return jnp.concatenate([docs * zeros] * HQ, axis=1)

    def keys_of(kv, i):
        return kv[pl.ds(i * KS, KS), :, :HD].reshape(KEYS, HD)

    def values_of(kv, i):
        return kv[pl.ds(i * KS, KS), :, HD:].reshape(KEYS, HD)

    def tops(kv, queries, start):
        def step(i, top):
            scores = dot(keys_of(kv, i), queries, NT) * SCALE
            k_pos = (
                i * KEYS + lax.broadcasted_iota(jnp.int32, (KEYS, HQ * TOK), 0)
            ).astype(F32)
            scores = jnp.where((k_pos >= start) & (k_pos <= q_pos), scores, -1e30)
            probs[i] = scores
            return jnp.maximum(top, jnp.max(scores, axis=0, keepdims=True))

        return lax.fori_loop(0, NK, step, jnp.full((1, HQ * TOK), -1e30, F32))

    def attended(kv, top):
        def step(i, carry):
            total, accum = carry
            p = jnp.exp(probs[i] - top)
            probs[i] = p
            total = total + jnp.sum(p, axis=0, keepdims=True)
            return total, accum + dot(values_of(kv, i), p.astype(B16), TN)

        total, accum = lax.fori_loop(
            0, NK, step, (jnp.zeros((1, HQ * TOK), F32), jnp.zeros((HD, HQ * TOK), F32))
        )
        return total, (accum / total).astype(B16)

    top = tops(kvb, q_b, starts(docs_b, 1))
    denom, att_cols = attended(kvb, top)
    att_cols = att_cols.astype(F32)
    att = from_columns(att_cols).astype(B16)

    @pl.loop(0, NG)
    def _(g):
        gm[g] = dot(grads[...], cd_of(g), NT) * ENC * g2(g)

    fore.x_near(0)
    fore.y_near()

    def mix_b(g, carry):
        squares, cross = carry
        mixed = sv[g].astype(F32) + dot(att, wo_of(g), NT)
        mx[g] = mixed
        return squares + row_sum(mixed * mixed), cross + row_sum(mixed * gm[g])

    squares, cross = lax.fori_loop(0, NG, mix_b, (zero, zero))
    r2b = rms_of(squares)
    lean = r2b * r2b * cross * (1.0 / D)
    fore.y_far()

    def grad_mix(g, total):
        grad = r2b * (gm[g] - mx[g] * lean)
        gm[g] = grad
        return total + dot(grad.astype(B16), wo_of(g), NN)

    grad_att = lax.fori_loop(0, NG, grad_mix, jnp.zeros((TOK, QW), F32)).astype(B16)
    g_heads = stack_heads(grad_att)
    delta = jnp.sum(to_columns(grad_att.astype(F32)) * att_cols, axis=0, keepdims=True)
    inverse = 1.0 / denom

    def backward_step(i, total):
        p = probs[i] * inverse
        grad_p = dot(values_of(kvb, i), g_heads, NT)
        grad_s = (p * (grad_p - delta) * SCALE).astype(B16)
        chips = pl.ds(i * (KS // NC), KS // NC)
        shape = (KS // NC, NC, TOK, HD)
        terms[chips, :, :, :HD] = dot(grad_s, q_b, NN).astype(B16).reshape(shape)
        terms[chips, :, :, HD:] = dot(p.astype(B16), g_heads, NN).astype(B16).reshape(shape)
        return total + dot(keys_of(kvb, i), grad_s, TN)

    grad_q = jnp.zeros((HD, HQ * TOK), F32)
    per = NK // NG

    def backward(dx, total):
        g = lax.rem(me.x + (dx + NX), NX)
        total = lax.fori_loop(g * per, (g + 1) * per, backward_step, total)
        scatter.send_pair(dx)
        return total

    grad_q = backward(2, grad_q)
    fore.x_near(-1)
    grad_q = backward(1, grad_q)
    scatter.add_pair(2)
    scatter.x_start()
    fore.x_near(1)
    grad_q = backward(-1, grad_q)
    scatter.add_pair(1)
    scatter.x_up()
    fore.x_near(2)
    grad_q = backward(0, grad_q)
    scatter.add_pair(-1)
    scatter.x_down()
    scatter.x_far()
    fore.x_far(*everyone)
    scatter.add_pair(0)
    grad_q = from_columns(grad_q).astype(B16)
    fore.end()

    top = tops(kvf, q_f, starts(docs_f, 0))
    scatter.along_y()
    _, att_cols = attended(kvf, top)
    att = from_columns(att_cols.astype(F32)).astype(B16)
    scatter.y_far()

    def mix_f(g, total):
        mixed = st[g] + dot(att, wo_of(g), NT)
        st[g] = mixed
        return total + row_sum(mixed * mixed)

    r2f = rms_of(lax.fori_loop(0, NG, mix_f, zero))

    def encode(g, total):
        normed = (st[g] * r2f * g2(g)).astype(B16)
        return total + dot(normed, cd_of(g), NN)

    coded = lax.fori_loop(0, NG, encode, jnp.zeros((TOK, R), F32))
    sent[...] = (coded * ENC).astype(B16)
    wire.send(sent, codes_out, after, codes_sent, codes_in)

    kv_grad = scatter.result().astype(B16)

    def grad_norm(g, total):
        weighted = (dot(grad_q, wq_of(g), NT) + dot(kv_grad, wk_of(g), NT)) * g1(g)
        mx[g] = weighted
        return total + row_sum(weighted * sv[g].astype(F32))

    cross = lax.fori_loop(0, NG, grad_norm, zero)
    lean1 = r1b * r1b * cross * (1.0 / D)

    def grad_code(g, total):
        grad = gm[g] + r1b * (mx[g] - sv[g].astype(F32) * lean1)
        return total + dot(grad.astype(B16), cd_of(g), NN)

    gin[...] = lax.fori_loop(0, NG, grad_code, jnp.zeros((TOK, R), F32)).astype(B16)
    wire.send(gin, grads_out, before, grads_sent, grads_in)
    for gather in (first, second, codec, metas, back, fore, scatter):
        gather.finish()
    wire.take(codes_sent, sent)
    wire.take(codes_in, codes_out)
    wire.take(grads_sent, gin)
    wire.take(grads_in, grads_out)


ANY = pl.BlockSpec(memory_space=pl.ANY)
VMEM = pl.BlockSpec(memory_space=pltpu.VMEM)


def on_device(
    codes_fwd, saved_stream, grad_codes, docs_fwd, docs_bwd, codec, wqkv, wout, gain_attn, gain_code
):
    half = NYH // 2
    codes, grads = pl.pallas_call(
        tick_kernel,
        out_shape=(jax.ShapeDtypeStruct((TOK, R), B16),) * 2,
        in_specs=[ANY, ANY, ANY, VMEM, VMEM, VMEM, ANY, ANY, VMEM, VMEM],
        out_specs=(VMEM, VMEM),
        scratch_shapes=[
            pltpu.VMEM((NSEQ, TOK, 2 * HD), B16),
            pltpu.VMEM((NSEQ, TOK, 2 * QW), B16),
            pltpu.VMEM((D, R), B16),
            pltpu.VMEM((NC, NX * NYH, 8, TOK), F32),
            pltpu.VMEM((NG, 8, GW), F32),
            pltpu.VMEM((NG, TOK, GW), B16),
            pltpu.VMEM((NG, TOK, GW), B16),
            pltpu.VMEM((NG, TOK, GW), F32),
            pltpu.VMEM((NG, TOK, GW), F32),
            pltpu.VMEM((NG, TOK, GW), F32),
            pltpu.VMEM((NSEQ, TOK, 2 * HD), B16),
            pltpu.VMEM((NSEQ, TOK, 2 * HD), B16),
            pltpu.VMEM((NK, KEYS, HQ * TOK), F32),
            pltpu.VMEM((NX * NYH, NC, TOK, 2 * HD), B16),
            pltpu.VMEM((TOK, R), B16),
            pltpu.VMEM((TOK, R), B16),
            pltpu.VMEM((TOK, R), B16),
            pltpu.VMEM((TOK, R), B16),
            pltpu.VMEM((CROWS, R), B16),
            pltpu.VMEM((CROWS, R), B16),
            pltpu.VMEM((CROWS, R), B16),
            pltpu.VMEM((NX * NYH, TOK, 2 * HD), B16),
            pltpu.VMEM((NX * NYH, TOK, 2 * HD), B16),
            pltpu.VMEM((half, TOK, 2 * HD), B16),
            pltpu.VMEM((half, TOK, 2 * HD), B16),
            pltpu.VMEM((NYH, TOK, 2 * HD), B16),
            pltpu.VMEM((NYH, TOK, 2 * HD), B16),
            pltpu.VMEM((NYH, TOK, 2 * HD), B16),
            pltpu.VMEM((TOK // 2, 2 * HD), B16),
            pltpu.VMEM((TOK // 2, 2 * HD), B16),
            pltpu.VMEM((TOK, 2 * HD), B16),
            pltpu.VMEM((TOK, 2 * HD), B16),
            pltpu.SemaphoreType.DMA((SEMAPHORES,)),
            pltpu.SemaphoreType.DMA((10,)),
        ],
        compiler_params=pltpu.CompilerParams(
            collective_id=0, has_side_effects=True, vmem_limit_bytes=56 * 2**20
        ),
        name="tick",
    )(
        codes_fwd[0], saved_stream[0], grad_codes[0], docs_fwd, docs_bwd, codec, wqkv, wout,
        gain_attn, gain_code,
    )
    return codes[None], grads[None]


def solution(mesh):
    return jax.shard_map(
        on_device,
        mesh=mesh,
        in_specs=(
            P("section", "seq", None),
            P("section", "seq", None),
            P("section", "seq", None),
            P("section", "seq"),
            P("section", "seq"),
            P(("section", "seq"), None),
            P("section", "seq", None),
            P("section", "seq", None),
            P("section", "seq"),
            P("section", "seq"),
        ),
        out_specs=(P("section", "seq", None), P("section", "seq", None)),
        check_vma=False,
    )
```

time: 124 us -> 113 us (0.911); the launches traced: 122 us -> 113 us
  Pallas kernels: 119 us -> 110 us
    pallas_call x1, Pallas kernels: 119 us -> 110 us  [on_device(): pl.pallas_call(tick_kernel, out_shape=(jax.ShapeDtypeStruct((TOK, R), B16...]
where the time goes in v3:
time: 113 us
  Pallas kernels  110 us (97%)
  local copies, waits for them, and re-layouts  2.26 us (2%)
    pallas_call x1, Pallas kernels, on_device(): pl.pallas_call(tick_kernel, out_shape=(jax.ShapeDtypeStruct((TOK, R), B16...  110 us
    unnamed x4, local copies, waits for them, and re-layouts  2.26 us

profile of v3, /device:TPU:1, one launch (start us, length us, event | category | flops | bytes accessed | tf_op | source)
XLA Modules:
  0.0 112.7 jit_solution(8340367520805964573)
XLA Ops:
  0.6 109.8 %tick.1 = (bf16[128,512]{1,0:T(8,128)(2,1)}, bf16[128,512]{1,0:T(8,128)(2,1)}) custom-call(bf16[128,512]{1,0:T(8,128)(2,1)} %bitcast.6, bf16[128,4096]{1,0:T(8,128)(2,1)} %bitcast.5, bf16[128,512]{1,0:T(8,128)(2,1)} %bitcast.7, s32[1,128]{1,0:T(1,128)} %docs_f_ref.1, s32[1,128]{1,0:T(1,128)} %docs_b_ref.1, bf16[8,512]{1,0:T(8,128)(2,1)} %codec_ref.1, ...), custom_call_target="tpu_custom_call" | custom-call | tf_op jit(solution)/shard_map/tick/pallas_call | solution.py:800
  110.4 0.0 copy-start
  110.5 1.6 %copy.14 = bf16[1,128,512]{2,1,0:T(8,128)(2,1)} copy(bf16[1,128,512]{2,1,0:T(8,128)(2,1)} %bitcast.9) | data formatting | bytes 262144
  112.1 0.0 copy-done
  112.1 0.7 copy.15
Async XLA Ops:
  110.4 1.6 %copy-start = (bf16[128,512]{1,0:T(8,128)(2,1)S(1)}, bf16[128,512]{1,0:T(8,128)(2,1)}, u32[]{:S(2)}) copy-start(bf16[128,512]{1,0:T(8,128)(2,1)} %get-tuple-element.5) | copy-start | bytes 393220

commit v4 on v3

--- a/solution.py
+++ b/solution.py
@@ -620,8 +620,10 @@
     codec.end()
 
     def decode(g, total):
-        stream = dot(codes[...], cd_of(g), NT)
+        wide = dot(jnp.concatenate([codes[...], grads[...]], axis=0), cd_of(g), NT)
+        stream = wide[:TOK]
         st[g] = stream
+        gm[g] = wide[TOK:] * ENC * g2(g)
         return total + row_sum(stream * stream)
 
     r1f = rms_of(lax.fori_loop(0, NG, decode, zero))
@@ -632,7 +634,6 @@
 
     kvf[own] = project(nb, wk_of)
     fore.begin()
-    q_f = stack_heads(project(nb, wq_of))
     back.end()
 
     q_pos = (own * TOK + lax.broadcasted_iota(jnp.int32, (1, TOK), 1)).astype(F32)
@@ -677,10 +678,6 @@
     denom, att_cols = attended(kvb, top)
     att_cols = att_cols.astype(F32)
     att = from_columns(att_cols).astype(B16)
-
-    @pl.loop(0, NG)
-    def _(g):
-        gm[g] = dot(grads[...], cd_of(g), NT) * ENC * g2(g)
 
     fore.x_near(0)
     fore.y_near()
@@ -742,6 +739,7 @@
     fore.x_far(*everyone)
     scatter.add_pair(0)
     grad_q = from_columns(grad_q).astype(B16)
+    q_f = stack_heads(project(nb, wq_of))
     fore.end()
 
     top = tops(kvf, q_f, starts(docs_f, 0))

time: 113 us -> 110 us (0.973)
  Pallas kernels: 110 us -> 107 us
    pallas_call x1, Pallas kernels: 110 us -> 107 us  [on_device(): pl.pallas_call(tick_kernel, out_shape=(jax.ShapeDtypeStruct((TOK, R), B16...]
where the time goes in v4:
time: 110 us
  Pallas kernels  107 us (97%)
  local copies, waits for them, and re-layouts  2.26 us (2%)
    pallas_call x1, Pallas kernels, on_device(): pl.pallas_call(tick_kernel, out_shape=(jax.ShapeDtypeStruct((TOK, R), B16...  107 us
    unnamed x4, local copies, waits for them, and re-layouts  2.26 us

profile of v4, /device:TPU:1, one launch (start us, length us, event | category | flops | bytes accessed | tf_op | source)
XLA Modules:
  0.0 109.6 jit_solution(7691567043254447642)
XLA Ops:
  0.6 106.7 %tick.1 = (bf16[128,512]{1,0:T(8,128)(2,1)}, bf16[128,512]{1,0:T(8,128)(2,1)}) custom-call(bf16[128,512]{1,0:T(8,128)(2,1)} %bitcast.6, bf16[128,4096]{1,0:T(8,128)(2,1)} %bitcast.5, bf16[128,512]{1,0:T(8,128)(2,1)} %bitcast.7, s32[1,128]{1,0:T(1,128)} %docs_f_ref.1, s32[1,128]{1,0:T(1,128)} %docs_b_ref.1, bf16[8,512]{1,0:T(8,128)(2,1)} %codec_ref.1, ...), custom_call_target="tpu_custom_call" | custom-call | tf_op jit(solution)/shard_map/tick/pallas_call | solution.py:798
  107.3 0.0 copy-start
  107.3 1.6 %copy.14 = bf16[1,128,512]{2,1,0:T(8,128)(2,1)} copy(bf16[1,128,512]{2,1,0:T(8,128)(2,1)} %bitcast.9) | data formatting | bytes 262144
  108.9 0.0 copy-done
  108.9 0.7 copy.15
Async XLA Ops:
  107.3 1.6 %copy-start = (bf16[128,512]{1,0:T(8,128)(2,1)S(1)}, bf16[128,512]{1,0:T(8,128)(2,1)}, u32[]{:S(2)}) copy-start(bf16[128,512]{1,0:T(8,128)(2,1)} %get-tuple-element.5) | copy-start | bytes 393220
